TPU v7x, 256 devices: a whole 4x4x8 slice. The times are simulated.
256 devices in a mesh: vocab: 64 (over z, x, core), rows: 4 (over y).
Axes of the slice: x: 4, y: 4, z: 8, core: 2. Of those that a mesh axis runs over, the one named last changes fastest.
Arguments:
- hidden: bfloat16 [1024, 4096], P(('vocab', 'rows')), may hold values from -6 to 6, as said below
- head: bfloat16 [81920, 4096], P('vocab'), as said below
- row_weight: float32 [1024], P(('vocab', 'rows')), may hold values from 30 to 300
- teacher_ids: int32 [1024, 128], P(('vocab', 'rows')), may hold values from 0 to 81919, as said below
- teacher_probs: int32 [1024, 128], P(('vocab', 'rows')), may hold values from 1 to 65409, as said below
Outputs:
- row_grad: bfloat16 [1024, 4096], P(('vocab', 'rows'))
- row_loss: float32 [1024], P(('vocab', 'rows'))
- head_grad: bfloat16 [4096, 81920], P('rows', 'vocab')
Inputs may be any that keep to these rules, and one draw needn't show every extreme that they name: `teacher_ids`: each row names 128 different ids. The 4 rows of one device (an aligned block) name at most 16 ids in any one vocabulary shard (ids s * 1280 to (s + 1) * 1280 - 1), and exactly 16 in one shard. `teacher_probs`: each row's 128 values sum to exactly 65536. `hidden`: entries of order one. `head`: entries of order 3 / sqrt(4096).
All inputs are finite; a program needn't handle non-finite values.
Results may differ from a plain program's by a relative error of at most 0.024.
Values may be sent and summed in bfloat16 or wider, within the bound.
A program may use at most 128 MiB of HBM per device.

v0:
```python
import jax
import jax.numpy as jnp
from jax import lax
from jax.sharding import PartitionSpec as P


def shards(hidden, head, row_weight, teacher_ids, teacher_probs):
    own_rows = hidden.shape[0]
    shard_width = head.shape[0]
    shard_count = lax.axis_size("vocab")
    position = lax.axis_index("vocab")
    group_rows = own_rows * shard_count
    group_hidden, group_weight = (
        lax.all_gather(hidden, "vocab", axis=0, tiled=True),
        lax.all_gather(row_weight.astype(jnp.bfloat16), "vocab", axis=0, tiled=True).astype(
            row_weight.dtype
        ),
    )
    logits = lax.dot_general(
        group_hidden, head, (((1,), (1,)), ((), ())), preferred_element_type=jnp.float32
    )
    local_max = jnp.max(logits, axis=1)
    row_max = lax.pmax(local_max, "vocab")
    shifted = jnp.exp(logits - row_max[:, None])
    row_total = lax.psum(jnp.sum(shifted, axis=1), "vocab")
    empty_teacher = jnp.zeros((group_rows, shard_width), jnp.float32)
    group_ids, group_probs = (
        lax.all_gather(teacher_ids, "vocab", axis=0, tiled=True),
        lax.all_gather(teacher_probs, "vocab", axis=0, tiled=True),
    )
    owners = group_ids // shard_width
    offset = group_ids - owners * shard_width
    is_mine = owners == position
    row_index = jnp.broadcast_to(jnp.arange(group_rows, dtype=jnp.int32)[:, None], group_ids.shape)
    values = jnp.where(is_mine, group_probs.astype(jnp.float32) / 65536.0, 0.0)
    teacher = empty_teacher.at[row_index, offset].add(values)
    teacher_dot = jnp.sum(teacher * logits, axis=1)
    grad_logits = (group_weight[:, None] * (shifted / row_total[:, None] - teacher)).astype(
        jnp.bfloat16
    )
    partial_rows = jnp.dot(grad_logits, head, preferred_element_type=jnp.float32)
    row_grad, teacher_term = (
        lax.psum_scatter(partial_rows, "vocab", scatter_dimension=0, tiled=True),
        lax.psum_scatter(teacher_dot, "vocab", scatter_dimension=0, tiled=True),
    )
    own_max = lax.dynamic_slice_in_dim(row_max, position * own_rows, own_rows)
    own_total = lax.dynamic_slice_in_dim(row_total, position * own_rows, own_rows)
    row_loss = own_max + jnp.log(own_total) - teacher_term
    head_grad = lax.psum_scatter(
        lax.dot_general(
            group_hidden, grad_logits, (((0,), (0,)), ((), ())), preferred_element_type=jnp.float32
        ).astype(jnp.bfloat16),
        "rows",
        scatter_dimension=0,
        tiled=True,
    )
    return (row_grad.astype(jnp.bfloat16), row_loss, head_grad)


def solution(mesh):
    in_specs = (
        P(("vocab", "rows"), None),
        P("vocab", None),
        P(("vocab", "rows")),
        P(("vocab", "rows"), None),
        P(("vocab", "rows"), None),
    )
    out_specs = (P(("vocab", "rows"), None), P(("vocab", "rows")), P("rows", "vocab"))
    return jax.shard_map(shards, mesh=mesh, in_specs=in_specs, out_specs=out_specs, check_vma=False)
```

profile of v0, /device:TPU:2, one launch (start us, length us, event | category | flops | bytes accessed | tf_op | source)
XLA Modules:
  0.0 1042.0 jit_solution(9831342172882258994)
XLA Ops:
  7.2 0.0 all-gather.5.cloned.1.call-start
  7.2 0.7 all-gather.5.cloned.1.call-update
  7.9 0.0 reduce-scatter.2.cloned.1.call-start
  8.0 0.7 convert_element_type.21
  8.6 1.3 fusion.7
  10.6 0.2 dynamic-update-slice
  10.9 126.6 %all-reduce = bf16[256]{0:T(256)(128)(2,1)S(1)} all-reduce(bf16[256]{0:T(256)(128)(2,1)S(1)} %dynamic-update-slice), channel_id=1, replica_groups=mesh['vocab'=64,'rows'=4] {'vocab'}, use_global_device_ids=true, to_apply=%add | all-reduce | flops 256 | bytes 1024
  137.5 51.9 %all-gather.1 = s32[64,4,128]{2,1,0:T(4,128)S(1)} all-gather(s32[1,4,128]{2,1,0:T(4,128)} %bitcast.23), channel_id=1, replica_groups=mesh['vocab'=64,'rows'=4] {'vocab'}, dimensions={0}, use_global_device_ids=true | all-gather | bytes 133120 | tf_op jit(solution)/shard_map/all_gather | solution.py:28
  189.4 47.0 %all-gather.2 = s32[64,4,128]{2,1,0:T(4,128)S(1)} all-gather(s32[1,4,128]{2,1,0:T(4,128)} %bitcast.24), channel_id=1, replica_groups=mesh['vocab'=64,'rows'=4] {'vocab'}, dimensions={0}, use_global_device_ids=true | all-gather | bytes 133120 | tf_op jit(solution)/shard_map/all_gather | solution.py:29
  236.4 0.1 fusion.4
  236.6 0.8 multiply_reduce_fusion.1
  237.3 0.8 and_reduce_fusion
  238.2 0.1 select_bitcast_fusion.1
  238.3 223.7 %scatter_custom_fusion = f32[327680]{0:T(1024)S(1)} fusion(s32[32768]{0:T(1024)S(1)} %select_bitcast_fusion, f32[32768]{0:T(1024)S(1)} %select_bitcast_fusion.1, f32[]{:T(128)} %constant.12.clone.1), kind=kCustom, calls=%fused_computation.7 | custom fusion | flops 32768 | bytes 1310724
  461.9 0.2 reshape.24
  462.2 0.0 all-gather.5.cloned.1.call-done
  462.2 2.5 reshape.35
  464.8 7.9 fusion.8
  472.7 123.6 %pmax.7 = f32[256]{0:T(256)S(1)} all-reduce(f32[256]{0:T(256)S(1)} %get-tuple-element.15), channel_id=1, replica_groups=mesh['vocab'=64,'rows'=4] {'vocab'}, use_global_device_ids=true, to_apply=%region_1.0 | all-reduce | flops 256 | bytes 2048 | tf_op jit(solution)/shard_map/pmax | solution.py:23
  596.3 1.7 multiply_reduce_fusion
  598.0 124.0 %psum.7 = f32[256]{0:T(256)S(1)} all-reduce(f32[256]{0:T(256)S(1)} %get-tuple-element.10), channel_id=1, replica_groups=mesh['vocab'=64,'rows'=4] {'vocab'}, use_global_device_ids=true, to_apply=%region_3.0 | all-reduce | flops 256 | bytes 2048 | tf_op jit(solution)/shard_map/psum | solution.py:25
  722.1 7.2 fusion
  729.3 0.0 copy-start
  729.3 0.0 reduce-scatter.2.cloned.1.call-update
  730.1 0.6 copy-done
  730.6 8.8 fusion.6
  739.4 290.2 %all-reduce.5 = (bf16[256,4096]{1,0:T(8,128)(2,1)S(1)}, f32[256]{0:T(256)S(1)}) all-reduce(f32[256,4096]{1,0:T(8,128)} %fusion.6, f32[256]{0:T(256)S(1)} %get-tuple-element.9), channel_id=2, replica_groups=mesh['vocab'=64,'rows'=4] {'vocab'}, use_global_device_ids=true, to_apply=%region_5.6.clone | all-reduce | flops 1048832 | bytes 6293504
  1029.6 0.6 dynamic-slice_subtract_fusion
  1030.2 0.6 dynamic-slice_convert_fusion
  1030.8 0.0 reduce-scatter.2.cloned.1.call-done
  1030.8 4.4 copy.9
  (5 shorter events, 0.1 us)
Async XLA Ops:
  7.2 455.0 %all-gather.5.cloned.1.call-start = ((), (), s32[]{:S(2)}) async-start(), calls=%async_computation.2 | async-start | bytes 2129920 | tf_op jit(solution)/shard_map/all_gather | solution.py:14
  7.9 1022.9 %reduce-scatter.2.cloned.1.call-start = ((), (), s32[]{:S(2)}) async-start(), calls=%async_computation.1 | async-start | bytes 13107200 | tf_op jit(solution)/shard_map/reduce_scatter | solution.py:49
  729.3 1.3 copy-start
Sparse Core Ops, SparseCore 0:
  10.8 79.2 all-gather.4
  729.4 99.6 reduce-scatter.1
where the time goes:
time: 1050 us; the launch traced here: 1040 us
  blocking collectives  763 us (73%)
  other arithmetic  228 us (22%)
  matrix products  23.9 us (2%)
  between operations  15.5 us (1%)
    unnamed x2, blocking collectives  417 us
    unnamed x4, other arithmetic  225 us
    psum x1, blocking collectives, shards(): row_total = lax.psum(jnp.sum(shifted, axis=1), 'vocab')  124 us
    pmax x1, blocking collectives, shards(): row_max = lax.pmax(local_max, 'vocab')  124 us
    all_gather x1, blocking collectives, shards(): lax.all_gather(teacher_ids, 'vocab', axis=0, tiled=True)  51.9 us
    all_gather x1, blocking collectives, shards(): lax.all_gather(teacher_probs, 'vocab', axis=0, tiled=True)  47 us
  transfers between devices with their start and end apart: 2, of which 0 were waited for; matrix products, arithmetic and copies ran while one was open for 23% of the time, Pallas kernels for 0%

commit v1 on v0

v1 whole, which is shorter than its diff:
```python
import jax
import jax.numpy as jnp
from jax import lax
from jax.experimental import pallas as pl
from jax.experimental.pallas import tpu as pltpu
from jax.sharding import PartitionSpec as P

MESH = pl.DeviceIdType.MESH
BF, F32, I32 = jnp.bfloat16, jnp.float32, jnp.int32
NZ, NX, NC, NY = 8, 4, 2, 4
D, VOC, TOPK = 4096, 1280, 128
GRP = 256
SLOTS = 16
DS = D // NY
Q = 4
QW = D // Q
YC = 2
YW = VOC // YC


def iota(shape, dim):
    return lax.broadcasted_iota(I32, shape, dim)


def kernel(
    hidden, head_hbm, weight, ids, probs,
    row_out, loss_out, head_out,
    head, own16, xbuf, hid, meta_own, meta, hy,
    logits, e_buf, teacher, packet, st1, st2, cols,
    g_buf, gp, part, p_send, p_recv, s1, x_send, x_recv, z_f32, z_send, z_recv,
    acc, stage,
    sem_head, sem_out,
    x_s, x_r, xm_s, xm_r, ring_s, ring_r, zm_s, zm_r, sib_s, sib_r, sm_s, sm_r,
    hy_s, hy_r, hs_s, hs_r, st1_s, st1_r, st2_s, st2_r, y_s, y_r,
    rp_s, rp_r, rx_s, rx_r, rz_s, rz_r,
):
    v, y = lax.axis_index("vocab"), lax.axis_index("rows")
    z, x, c = lax.div(v, 8), lax.rem(lax.div(v, 2), 4), lax.rem(v, 2)
    oc = 1 - c

    def dev(dz=0, dx=0, dc=0, dy=0):
        zz = lax.rem(z + dz, NZ)
        xx = lax.rem(x + dx, NX)
        cc = c if dc == 0 else oc
        return (zz * 8 + xx * 2 + cc, lax.rem(y + dy, NY))

    started = []

    def send(src, dst, ss, rs, to):
        copy = pltpu.make_async_remote_copy(
            src_ref=src, dst_ref=dst, send_sem=ss, recv_sem=rs, device_id=to, device_id_type=MESH
        )
        copy.start()
        started.append(copy)
        return copy

    head_in = []
    for i in range(5):
        part_rows = pl.ds(i * 256, 256)
        copy = pltpu.make_async_copy(head_hbm.at[part_rows], head.at[part_rows], sem_head.at[i])
        copy.start()
        head_in.append(copy)

    xc = [(dx, dc) for dx in range(NX) for dc in range(NC) if (dx, dc) != (0, 0)]
    barrier = pltpu.get_barrier_semaphore()
    peers = [dev(dx=dx, dc=dc) for dx, dc in xc]
    peers += [dev(dz=d) for d in range(1, NZ)]
    peers += [dev(dy=d) for d in range(1, NY)]
    for to in peers:
        pl.semaphore_signal(barrier, inc=1, device_id=to, device_id_type=MESH)

    h = hidden[...].astype(F32)
    own16[...] = jnp.concatenate([h[:, q * QW:(q + 1) * QW] for q in range(Q)], axis=0).astype(BF)
    meta_own[0:4, :] = ids[...]
    meta_own[4:8, :] = probs[...]
    pl.semaphore_wait(barrier, len(peers))

    got = [send(own16, xbuf.at[x], x_s.at[d - 1], x_r.at[d - 1], dev(dx=d)) for d in (1, 3, 2)]
    base = c * 8 + z
    blk = base * 4 + x
    got_m = [send(meta_own, meta.at[blk], xm_s.at[d - 1], xm_r.at[d - 1], dev(dx=d)) for d in (1, 3, 2)]
    xbuf[x] = own16[...]
    meta[blk] = meta_own[...]
    for copy in got:
        copy.wait_recv()
    row0 = pl.multiple_of(base * 16, 16)
    blocks = [xbuf[i].astype(F32) for i in range(NX)]
    for q in range(Q):
        hid[pl.ds(row0, 16), q * QW:(q + 1) * QW] = jnp.concatenate(
            [b[4 * q:4 * q + 4] for b in blocks], axis=0
        ).astype(BF)

    def tile(zz):
        return hid.at[pl.ds(pl.multiple_of((c * 8 + zz) * 16, 16), 16)]

    def ring_send(way, step):
        zz = lax.rem(z + (NZ - step if way == 0 else step), NZ)
        ref = tile(zz)
        return send(ref, ref, ring_s.at[way, step], ring_r.at[way, step], dev(dz=1 if way == 0 else NZ - 1))

    sib = []

    def sib_send(zz):
        ref, n = tile(zz), len(sib)
        sib.append(send(ref, ref, sib_s.at[n], sib_r.at[n], dev(dc=1)))

    now = [ring_send(0, 0), ring_send(1, 0)]
    sib_send(z)
    for copy in got_m:
        copy.wait_recv()

    def meta_tile(zz):
        return meta.at[pl.ds((c * 8 + zz) * 4, 4)]

    own_meta = meta_tile(z)
    got_m = [send(own_meta, own_meta, zm_s.at[d - 1], zm_r.at[d - 1], dev(dz=d)) for d in range(1, NZ)]
    for step in range(1, 5):
        for way in range(2):
            if way == 1 and step == 4:
                continue
            now[way].wait_recv()
            if step < (4 if way == 0 else 3):
                now[way] = ring_send(way, step)
            sib_send(lax.rem(z + (NZ - step if way == 0 else step), NZ))

    half = pl.ds(pl.multiple_of(c * 128, 128), 128)
    got_hy = {}
    for d in (1, 3, 2):
        yy = lax.rem(y + d, NY)
        src = hid.at[half, pl.ds(pl.multiple_of(yy * DS, DS), DS)]
        got_hy[d] = send(src, hy.at[d - 1, half], hy_s.at[d - 1], hy_r.at[d - 1], dev(dy=d))

    for copy in got_m:
        copy.wait_recv()
    half_meta = meta.at[pl.ds(c * 32, 32)]
    got_sm = send(half_meta, half_meta, sm_s, sm_r, dev(dc=1))
    got_sm.wait_recv()

    first = v * VOC
    all_meta = meta[...]
    off = all_meta[:, 0:4, :].reshape(GRP, TOPK) - first
    prob = all_meta[:, 4:8, :].reshape(GRP, TOPK)
    mine = jnp.logical_and(off >= 0, off < VOC)
    mask = jnp.where(mine, 1.0, 0.0).astype(BF)
    before = jnp.where(iota((TOPK, TOPK), 0) < iota((TOPK, TOPK), 1), 1.0, 0.0).astype(BF)
    ri, rj = iota((GRP, GRP), 0), iota((GRP, GRP), 1)
    earlier = jnp.where(jnp.logical_and((ri >> 2) == (rj >> 2), rj < ri), 1.0, 0.0).astype(BF)
    count = jnp.dot(mask, jnp.ones((TOPK, TOPK), BF), preferred_element_type=F32).astype(BF)
    rank = jnp.dot(mask, before, preferred_element_type=F32)
    rank = rank + jnp.dot(earlier, count, preferred_element_type=F32)
    rank = jnp.where(mine, rank, -1.0).reshape(64, 4, TOPK)
    rows4 = iota((GRP, TOPK), 0) & 3
    code = (off * 4 + rows4).astype(F32).reshape(64, 4, TOPK)
    probf = prob.astype(F32).reshape(64, 4, TOPK)
    slot = iota((64, SLOTS, TOPK), 1).astype(F32)
    code_at = jnp.zeros((64, SLOTS, TOPK), F32)
    prob_at = jnp.zeros((64, SLOTS, TOPK), F32)
    for r in range(4):
        hit = rank[:, r:r + 1, :] == slot
        code_at = code_at + jnp.where(hit, code[:, r:r + 1, :], 0.0)
        prob_at = prob_at + jnp.where(hit, probf[:, r:r + 1, :], 0.0)
    code_i = jnp.sum(code_at, axis=2, keepdims=True).reshape(64 * SLOTS, 1).astype(I32)
    prob_i = jnp.sum(prob_at, axis=2, keepdims=True).reshape(64 * SLOTS, 1).astype(I32)
    lanes = iota((256, 128), 1)
    places = iota((256, VOC), 1)
    block_row = (iota((256, 128), 0) >> 4) << 2
    for b in range(4):
        code_b, prob_b = code_i[b * 256:(b + 1) * 256], prob_i[b * 256:(b + 1) * 256]
        one_hot = jnp.where((code_b >> 2) == places, 1.0, 0.0).astype(BF)
        byte = jnp.where(lanes < 64, prob_b >> 8, prob_b & 255).astype(F32)
        at = jnp.where((lanes & 63) == block_row + (code_b & 3), byte, 0.0).astype(BF)
        both = lax.dot_general(at, one_hot, (((0,), (0,)), ((), ())), preferred_element_type=F32)
        teacher[b * 64:(b + 1) * 64, :] = (both[0:64] * 256.0 + both[64:128]) * (1.0 / 65536.0)

    for copy in head_in:
        copy.wait()
    for copy in sib:
        copy.wait_recv()

    for n in range(5):
        ns = slice(n * 256, (n + 1) * 256)
        logits[:, ns] = lax.dot_general(
            hid[...], head[ns, :], (((1,), (1,)), ((), ())), preferred_element_type=F32
        )
    lg = logits[...]
    m_own = jnp.max(lg, axis=1, keepdims=True)
    ex = jnp.exp(lg - m_own)
    e_buf[...] = ex
    s_own = jnp.sum(ex, axis=1, keepdims=True)
    t_own = jnp.sum(teacher[...] * lg, axis=1, keepdims=True)
    my_row = blk * 4
    row_id = iota((GRP, 128), 0)
    lane = iota((GRP, 128), 1)
    w_own = jnp.zeros((GRP, 128), F32)
    for r in range(4):
        w_own = jnp.where(row_id == my_row + r, weight[r], w_own)
    wide = jnp.where(lane == 0, m_own, jnp.where(lane == 1, s_own, jnp.where(lane == 2, w_own, t_own)))
    packet[...] = wide.T[0:8, :]

    def combine(buf):
        top = buf[0, 0:1, :]
        for i in range(1, 8):
            top = jnp.maximum(top, buf[i, 0:1, :])
        total = [jnp.zeros((1, GRP), F32) for _ in range(3)]
        for i in range(8):
            total[0] = total[0] + buf[i, 1:2, :] * jnp.exp(buf[i, 0:1, :] - top)
            total[1] = total[1] + buf[i, 2:3, :]
            total[2] = total[2] + buf[i, 3:4, :]
        sub = iota((8, GRP), 0)
        return jnp.where(
            sub == 0, top, jnp.where(sub == 1, total[0], jnp.where(sub == 2, total[1], total[2]))
        )

    place = x * 2 + c
    got = [
        send(packet, st1.at[place], st1_s.at[i], st1_r.at[i], dev(dx=dx, dc=dc))
        for i, (dx, dc) in enumerate(xc)
    ]
    st1[place] = packet[...]
    for copy in got:
        copy.wait_recv()
    st2[z] = combine(st1)
    mid = st2.at[z]
    got = [send(mid, mid, st2_s.at[d - 1], st2_r.at[d - 1], dev(dz=d)) for d in range(1, NZ)]
    for copy in got:
        copy.wait_recv()
    final = combine(st2)
    cols[...] = jnp.concatenate([final, jnp.zeros((120, GRP), F32)], axis=0).T
    top_c, total_c, w_c = cols[:, 0:1], cols[:, 1:2], cols[:, 2:3]
    scale = jnp.exp(m_own - top_c) / total_c
    g_buf[0] = (w_c * (e_buf[...] * scale - teacher[...])).astype(BF)

    own_cols = cols[pl.ds(pl.multiple_of(my_row, 4), 4), :]
    loss_out[...] = own_cols[:, 0:1] + jnp.log(own_cols[:, 1:2]) - own_cols[:, 3:4] + jnp.zeros((4, 128), F32)

    got_y = {}
    for k in range(YC):
        ks = pl.ds(k * YW, YW)
        for d in (1, 3, 2):
            got_y[d, k] = send(
                g_buf.at[0, :, ks], g_buf.at[d, :, ks], y_s.at[d - 1, k], y_r.at[d - 1, k], dev(dy=d)
            )

    i0 = iota((GRP, GRP), 0)
    src = ((i0 >> 7) << 7) + (((i0 >> 2) & 7) << 4) + (((i0 >> 5) & 3) << 2) + (i0 & 3)
    perm = jnp.where(src == iota((GRP, GRP), 1), 1.0, 0.0).astype(BF)
    gp[...] = jnp.dot(perm, g_buf[0], preferred_element_type=F32).astype(BF)
    other = pl.ds(pl.multiple_of(oc * 128, 128), 128)
    got_p, got_x, got_z = {}, {}, {}

    def pair_stage(q):
        part[q % 2] = jnp.dot(gp[...], head[:, q * QW:(q + 1) * QW], preferred_element_type=F32)
        p_send[q] = part[q % 2, other, :].astype(BF)
        got_p[q] = send(p_send.at[q], p_recv.at[q], rp_s.at[q], rp_r.at[q], dev(dc=1))

    def x_stage(q):
        got_p[q].wait_recv()
        s1[q] = part[q % 2, half, :] + p_recv[q].astype(F32)
        x_send[q] = s1[q].astype(BF)
        for d in (1, 3, 2):
            xx = lax.rem(x + d, NX)
            rows = pl.ds(pl.multiple_of(xx * 32, 32), 32)
            got_x[q, d] = send(
                x_send.at[q, rows], x_recv.at[q, d - 1], rx_s.at[q, d - 1], rx_r.at[q, d - 1], dev(dx=d)
            )

    def z_stage(q):
        for d in (1, 3, 2):
            got_x[q, d].wait_recv()
        s2 = s1[q, pl.ds(pl.multiple_of(x * 32, 32), 32), :]
        for d in range(3):
            s2 = s2 + x_recv[q, d].astype(F32)
        for zz in range(NZ):
            piece = jnp.concatenate([s2[4 * zz:4 * zz + 4, i * 256:(i + 1) * 256] for i in range(4)], axis=0)
            z_f32[q, zz] = piece
            z_send[q, zz] = piece.astype(BF)
        for d in range(1, NZ):
            zz = lax.rem(z + d, NZ)
            got_z[q, d] = send(
                z_send.at[q, zz], z_recv.at[q, d - 1], rz_s.at[q, d - 1], rz_r.at[q, d - 1], dev(dz=d)
            )

    def last_stage(q):
        for d in range(1, NZ):
            got_z[q, d].wait_recv()
        total = z_f32[q, z]
        for d in range(NZ - 1):
            total = total + z_recv[q, d].astype(F32)
        row_out[:, q * QW:(q + 1) * QW] = jnp.concatenate(
            [total[4 * i:4 * i + 4] for i in range(4)], axis=1
        ).astype(BF)

    def head_step(d, k):
        ks = slice(k * YW, (k + 1) * YW)
        if d == 0:
            left = hid[:, pl.ds(pl.multiple_of(y * DS, DS), DS)]
        else:
            left = hy[d - 1]
            got_y[d, k].wait_recv()
        term = lax.dot_general(
            left, g_buf[d, :, ks], (((0,), (0,)), ((), ())), preferred_element_type=F32
        )
        if d == 0:
            acc[:, ks] = term
        elif d != 2:
            acc[:, ks] += term
        else:
            stage[:, ks] = (acc[:, ks] + term).astype(BF)

    pair_stage(0)
    pair_stage(1)
    x_stage(0)
    pair_stage(2)
    x_stage(1)
    pair_stage(3)
    x_stage(2)
    x_stage(3)
    got_hs = []
    for d in (1, 3, 2):
        got_hy[d].wait_recv()
        ref = hy.at[d - 1, half]
        got_hs.append(send(ref, ref, hs_s.at[d - 1], hs_r.at[d - 1], dev(dc=1)))
    z_stage(0)
    z_stage(1)
    head_step(0, 0)
    head_step(0, 1)
    z_stage(2)
    z_stage(3)
    for copy in got_hs:
        copy.wait_recv()
    for d in (1, 3):
        for k in range(YC):
            head_step(d, k)
    for q in range(Q):
        last_stage(q)
    outs = []
    for k in range(YC):
        head_step(2, k)
        ks = pl.ds(k * YW, YW)
        copy = pltpu.make_async_copy(stage.at[:, ks], head_out.at[:, ks], sem_out.at[k])
        copy.start()
        outs.append(copy)
    for copy in started:
        copy.wait_send()
    for copy in outs:
        copy.wait()


def shards(hidden, head, row_weight, teacher_ids, teacher_probs):
    dma = pltpu.SemaphoreType.DMA
    vm = pltpu.VMEM
    any_spec = pl.BlockSpec(memory_space=pl.ANY)
    vm_spec = pl.BlockSpec(memory_space=pltpu.VMEM)
    row_grad, loss, head_grad = pl.pallas_call(
        kernel,
        out_shape=(
            jax.ShapeDtypeStruct((4, D), BF),
            jax.ShapeDtypeStruct((4, 128), F32),
            jax.ShapeDtypeStruct((DS, VOC), BF),
        ),
        in_specs=[vm_spec, any_spec, pl.BlockSpec(memory_space=pltpu.SMEM), vm_spec, vm_spec],
        out_specs=(vm_spec, vm_spec, any_spec),
        scratch_shapes=[
            vm((VOC, D), BF), vm((16, QW), BF), vm((NX, 16, QW), BF), vm((GRP, D), BF),
            vm((8, 128), I32), vm((64, 8, 128), I32), vm((3, GRP, DS), BF),
            vm((GRP, VOC), F32), vm((GRP, VOC), F32), vm((GRP, VOC), F32),
            vm((8, GRP), F32), vm((8, 8, GRP), F32), vm((8, 8, GRP), F32), vm((GRP, 128), F32),
            vm((4, GRP, VOC), BF), vm((GRP, VOC), BF), vm((2, GRP, QW), F32),
            vm((Q, 128, QW), BF), vm((Q, 128, QW), BF), vm((Q, 128, QW), F32),
            vm((Q, 128, QW), BF), vm((Q, 3, 32, QW), BF),
            vm((Q, NZ, 16, 256), F32), vm((Q, NZ, 16, 256), BF), vm((Q, NZ - 1, 16, 256), BF),
            vm((DS, VOC), F32), vm((DS, VOC), BF),
            dma((5,)), dma((YC,)),
            dma((3,)), dma((3,)), dma((3,)), dma((3,)), dma((2, 4)), dma((2, 4)),
            dma((7,)), dma((7,)), dma((8,)), dma((8,)), dma, dma,
            dma((3,)), dma((3,)), dma((3,)), dma((3,)), dma((7,)), dma((7,)), dma((7,)), dma((7,)),
            dma((3, YC)), dma((3, YC)),
            dma((Q,)), dma((Q,)), dma((Q, 3)), dma((Q, 3)), dma((Q, 7)), dma((Q, 7)),
        ],
        compiler_params=pltpu.CompilerParams(
            collective_id=0, has_side_effects=True, vmem_limit_bytes=60 << 20
        ),
        cost_estimate=pl.CostEstimate(flops=8_100_000_000, bytes_accessed=14_000_000, transcendentals=330_000),
    )(hidden, head, row_weight, teacher_ids, teacher_probs)
    return row_grad, loss[:, 0], head_grad


def solution(mesh):
    in_specs = (
        P(("vocab", "rows"), None),
        P("vocab", None),
        P(("vocab", "rows")),
        P(("vocab", "rows"), None),
        P(("vocab", "rows"), None),
    )
    out_specs = (P(("vocab", "rows"), None), P(("vocab", "rows")), P("rows", "vocab"))
    return jax.shard_map(shards, mesh=mesh, in_specs=in_specs, out_specs=out_specs, check_vma=False)
```

time: 1050 us -> 93.6 us (0.09)
  blocking collectives: 763 us -> 0 us
  other arithmetic: 228 us -> 0 us
  Pallas kernels: 0 us -> 86.6 us
  matrix products: 23.9 us -> 0 us
  between operations: 15.5 us -> 0.64 us
    unnamed x2 -> x0, blocking collectives: 417 us -> none
    unnamed x4 -> x0, other arithmetic: 225 us -> none
    psum x1 -> x0, blocking collectives: 124 us -> none  [shards(): row_total = lax.psum(jnp.sum(shifted, axis=1), 'vocab')]
    pmax x1 -> x0, blocking collectives: 124 us -> none  [shards(): row_max = lax.pmax(local_max, 'vocab')]
    all_gather x2 -> x0, blocking collectives: 99 us -> none  [the longest x1 51.9 us: shards(): lax.all_gather(teacher_ids, 'vocab', axis=0, tiled=True)]
    pallas_call x0 -> x1, Pallas kernels: none -> 86.6 us  [shards(): pl.pallas_call(kernel, out_shape=(jax.ShapeDtypeStruct((4, D), BF), jax.S...]
    dot_general x3 -> x0, matrix products: 23.9 us -> none  [the longest x1 8.78 us: shards(): jnp.dot(grad_logits, head, preferred_element_type=jnp.float32)]
  transfers between devices with their start and end apart: 2 -> 0, of which waited for: 0 -> 0; matrix products, arithmetic and copies ran while one was open for 23% -> 0% of each run, Pallas kernels for 0% -> 0%
where the time goes in v1:
time: 93.6 us; the launch traced here: 93.3 us
  Pallas kernels  86.6 us (93%)
  local copies, waits for them, and re-layouts  6.09 us (7%)
    pallas_call x1, Pallas kernels, shards(): pl.pallas_call(kernel, out_shape=(jax.ShapeDtypeStruct((4, D), BF), jax.S...  86.6 us
    unnamed x2, local copies, waits for them, and re-layouts  4.78 us

profile of v1, /device:TPU:2, one launch (start us, length us, event | category | flops | bytes accessed | tf_op | source)
XLA Modules:
  0.0 93.3 jit_solution(3732880209842259158)
XLA Ops:
  0.6 86.6 %shard_map.76 = (bf16[4,4096]{1,0:T(4,128)(2,1)}, f32[4,128]{1,0:T(4,128)}, bf16[1024,1280]{1,0:T(8,128)(2,1)}) custom-call(bf16[4,4096]{1,0:T(4,128)(2,1)} %hidden.1, bf16[1280,4096]{1,0:T(8,128)(2,1)} %head_hbm.1, f32[4]{0:T(128)} %weight.1, s32[4,128]{1,0:T(4,128)} %ids.1, s32[4,128]{1,0:T(4,128)} %probs.1), custom_call_target="tpu_custom_call" | custom-call | flops 8099999744 | bytes 14000000 | tf_op jit(solution)/shard_map/pallas_call | solution.py:354
  87.2 1.3 %slice_reduce_fusion = f32[4]{0:T(128)} fusion(f32[4,128]{1,0:T(4,128)} %get-tuple-element.7), kind=kLoop, calls=%fused_computation | loop fusion | bytes 32 | tf_op jit(solution)/shard_map/slice | solution.py:385
  88.5 1.4 %copy.10 = bf16[4,4096]{1,0:T(4,128)(2,1)} copy(bf16[4,4096]{1,0:T(4,128)(2,1)} %get-tuple-element.12) | data formatting | bytes 65536
  89.9 3.4 %copy.11 = bf16[1024,1280]{1,0:T(8,128)(2,1)} copy(bf16[1024,1280]{1,0:T(8,128)(2,1)} %get-tuple-element.14) | data formatting | bytes 5242880

commit v2 on v1

--- a/solution.py
+++ b/solution.py
@@ -14,6 +14,8 @@
 DS = D // NY
 Q = 4
 QW = D // Q
+DH = D // 2
+PW = DH // 4
 YC = 2
 YW = VOC // YC
 
@@ -25,13 +27,15 @@
 def kernel(
     hidden, head_hbm, weight, ids, probs,
     row_out, loss_out, head_out,
-    head, own16, xbuf, hid, meta_own, meta, hy,
-    logits, e_buf, teacher, packet, st1, st2, cols,
+    head, own_a, own_b, buf_a, buf_b, hid, meta_own, meta, hy,
+    logits, e_buf, teacher, packet, st1, st2, cols, packet2, td1, td2, dot_buf,
     g_buf, gp, part, p_send, p_recv, s1, x_send, x_recv, z_f32, z_send, z_recv,
     acc, stage,
     sem_head, sem_out,
-    x_s, x_r, xm_s, xm_r, ring_s, ring_r, zm_s, zm_r, sib_s, sib_r, sm_s, sm_r,
-    hy_s, hy_r, hs_s, hs_r, st1_s, st1_r, st2_s, st2_r, y_s, y_r,
+    xa_s, xa_r, zb_s, zb_r, xb_s, xb_r, xm_s, xm_r, ring_s, ring_r, zm_s, zm_r,
+    sib_s, sib_r, sm_s, sm_r,
+    hy_s, hy_r, hs_s, hs_r, st1_s, st1_r, st2_s, st2_r, td1_s, td1_r, td2_s, td2_r,
+    y_s, y_r, f_s, f_r,
     rp_s, rp_r, rx_s, rx_r, rz_s, rz_r,
 ):
     v, y = lax.axis_index("vocab"), lax.axis_index("rows")
@@ -70,50 +74,52 @@
         pl.semaphore_signal(barrier, inc=1, device_id=to, device_id_type=MESH)
 
     h = hidden[...].astype(F32)
-    own16[...] = jnp.concatenate([h[:, q * QW:(q + 1) * QW] for q in range(Q)], axis=0).astype(BF)
+    for own, at in ((own_a, 0), (own_b, DH)):
+        own[...] = jnp.concatenate(
+            [h[:, at + i * PW:at + (i + 1) * PW] for i in range(4)], axis=0
+        ).astype(BF)
     meta_own[0:4, :] = ids[...]
     meta_own[4:8, :] = probs[...]
     pl.semaphore_wait(barrier, len(peers))
 
-    got = [send(own16, xbuf.at[x], x_s.at[d - 1], x_r.at[d - 1], dev(dx=d)) for d in (1, 3, 2)]
+    got_a = [send(own_a, buf_a.at[x], xa_s.at[d - 1], xa_r.at[d - 1], dev(dx=d)) for d in (1, 3, 2)]
+    got_b = [send(own_b, buf_b.at[x, z], zb_s.at[d - 1], zb_r.at[d - 1], dev(dz=d)) for d in range(1, NZ)]
     base = c * 8 + z
     blk = base * 4 + x
     got_m = [send(meta_own, meta.at[blk], xm_s.at[d - 1], xm_r.at[d - 1], dev(dx=d)) for d in (1, 3, 2)]
-    xbuf[x] = own16[...]
+    buf_a[x] = own_a[...]
+    buf_b[x, z] = own_b[...]
     meta[blk] = meta_own[...]
-    for copy in got:
-        copy.wait_recv()
-    row0 = pl.multiple_of(base * 16, 16)
-    blocks = [xbuf[i].astype(F32) for i in range(NX)]
-    for q in range(Q):
-        hid[pl.ds(row0, 16), q * QW:(q + 1) * QW] = jnp.concatenate(
-            [b[4 * q:4 * q + 4] for b in blocks], axis=0
-        ).astype(BF)
-
-    def tile(zz):
-        return hid.at[pl.ds(pl.multiple_of((c * 8 + zz) * 16, 16), 16)]
+
+    def rows_of(zz):
+        return pl.ds(pl.multiple_of((c * 8 + zz) * 16, 16), 16)
+
+    def lay_out(blocks, zz, at):
+        blocks = [b.astype(F32) for b in blocks]
+        for i in range(4):
+            hid[rows_of(zz), at + i * PW:at + (i + 1) * PW] = jnp.concatenate(
+                [b[4 * i:4 * i + 4] for b in blocks], axis=0
+            ).astype(BF)
+
+    sib = []
+
+    def sib_send(zz, at):
+        ref, n = hid.at[rows_of(zz), at:at + DH], len(sib)
+        sib.append(send(ref, ref, sib_s.at[n], sib_r.at[n], dev(dc=1)))
 
     def ring_send(way, step):
         zz = lax.rem(z + (NZ - step if way == 0 else step), NZ)
-        ref = tile(zz)
+        ref = hid.at[rows_of(zz), 0:DH]
         return send(ref, ref, ring_s.at[way, step], ring_r.at[way, step], dev(dz=1 if way == 0 else NZ - 1))
 
-    sib = []
-
-    def sib_send(zz):
-        ref, n = tile(zz), len(sib)
-        sib.append(send(ref, ref, sib_s.at[n], sib_r.at[n], dev(dc=1)))
-
+    for copy in got_a:
+        copy.wait_recv()
+    lay_out([buf_a[i] for i in range(NX)], z, 0)
     now = [ring_send(0, 0), ring_send(1, 0)]
-    sib_send(z)
+    sib_send(z, 0)
     for copy in got_m:
         copy.wait_recv()
-
-    def meta_tile(zz):
-        return meta.at[pl.ds((c * 8 + zz) * 4, 4)]
-
-    own_meta = meta_tile(z)
-    got_m = [send(own_meta, own_meta, zm_s.at[d - 1], zm_r.at[d - 1], dev(dz=d)) for d in range(1, NZ)]
+    own_meta = meta.at[pl.ds((c * 8 + z) * 4, 4)]
     for step in range(1, 5):
         for way in range(2):
             if way == 1 and step == 4:
@@ -121,7 +127,20 @@
             now[way].wait_recv()
             if step < (4 if way == 0 else 3):
                 now[way] = ring_send(way, step)
-            sib_send(lax.rem(z + (NZ - step if way == 0 else step), NZ))
+            sib_send(lax.rem(z + (NZ - step if way == 0 else step), NZ), 0)
+        if step == 1:
+            for copy in got_b:
+                copy.wait_recv()
+            mine = buf_b.at[x]
+            got_b = [send(mine, mine, xb_s.at[d - 1], xb_r.at[d - 1], dev(dx=d)) for d in (1, 3, 2)]
+            got_m = [
+                send(own_meta, own_meta, zm_s.at[d - 1], zm_r.at[d - 1], dev(dz=d)) for d in range(1, NZ)
+            ]
+    for copy in got_b:
+        copy.wait_recv()
+    for zz in range(NZ):
+        lay_out([buf_b[i, zz] for i in range(NX)], zz, DH)
+        sib_send(zz, DH)
 
     half = pl.ds(pl.multiple_of(c * 128, 128), 128)
     got_hy = {}
@@ -134,6 +153,63 @@
         copy.wait_recv()
     half_meta = meta.at[pl.ds(c * 32, 32)]
     got_sm = send(half_meta, half_meta, sm_s, sm_r, dev(dc=1))
+
+    for copy in head_in:
+        copy.wait()
+    for copy in sib[:8]:
+        copy.wait_recv()
+    for n in range(5):
+        ns = slice(n * 256, (n + 1) * 256)
+        logits[:, ns] = lax.dot_general(
+            hid[:, 0:DH], head[ns, 0:DH], (((1,), (1,)), ((), ())), preferred_element_type=F32
+        )
+    for copy in sib[8:]:
+        copy.wait_recv()
+    for n in range(5):
+        ns = slice(n * 256, (n + 1) * 256)
+        logits[:, ns] += lax.dot_general(
+            hid[:, DH:D], head[ns, DH:D], (((1,), (1,)), ((), ())), preferred_element_type=F32
+        )
+    lg = logits[...]
+    m_own = jnp.max(lg, axis=1, keepdims=True)
+    ex = jnp.exp(lg - m_own)
+    e_buf[...] = ex
+    s_own = jnp.sum(ex, axis=1, keepdims=True)
+    my_row = blk * 4
+    row_id = iota((GRP, 128), 0)
+    lane = iota((GRP, 128), 1)
+    w_own = jnp.zeros((GRP, 128), F32)
+    for r in range(4):
+        w_own = jnp.where(row_id == my_row + r, weight[r], w_own)
+    wide = jnp.where(lane == 0, m_own, jnp.where(lane == 1, s_own, w_own))
+    packet[...] = wide.T[0:8, :]
+
+    def combine(buf):
+        top = buf[0, 0:1, :]
+        for i in range(1, 8):
+            top = jnp.maximum(top, buf[i, 0:1, :])
+        total = [jnp.zeros((1, GRP), F32) for _ in range(2)]
+        for i in range(8):
+            total[0] = total[0] + buf[i, 1:2, :] * jnp.exp(buf[i, 0:1, :] - top)
+            total[1] = total[1] + buf[i, 2:3, :]
+        sub = iota((8, GRP), 0)
+        return jnp.where(sub == 0, top, jnp.where(sub == 1, total[0], total[1]))
+
+    place = x * 2 + c
+
+    def over_xc(own, buf, ss, rs):
+        got = [
+            send(own, buf.at[place], ss.at[i], rs.at[i], dev(dx=dx, dc=dc))
+            for i, (dx, dc) in enumerate(xc)
+        ]
+        buf[place] = own[...]
+        return got
+
+    def over_z(buf, ss, rs):
+        mid = buf.at[z]
+        return [send(mid, mid, ss.at[d - 1], rs.at[d - 1], dev(dz=d)) for d in range(1, NZ)]
+
+    got = over_xc(packet, st1, st1_s, st1_r)
     got_sm.wait_recv()
 
     first = v * VOC
@@ -159,6 +235,10 @@
         hit = rank[:, r:r + 1, :] == slot
         code_at = code_at + jnp.where(hit, code[:, r:r + 1, :], 0.0)
         prob_at = prob_at + jnp.where(hit, probf[:, r:r + 1, :], 0.0)
+    for copy in got:
+        copy.wait_recv()
+    st2[z] = combine(st1)
+    got = over_z(st2, st2_s, st2_r)
     code_i = jnp.sum(code_at, axis=2, keepdims=True).reshape(64 * SLOTS, 1).astype(I32)
     prob_i = jnp.sum(prob_at, axis=2, keepdims=True).reshape(64 * SLOTS, 1).astype(I32)
     lanes = iota((256, 128), 1)
@@ -172,56 +252,8 @@
         both = lax.dot_general(at, one_hot, (((0,), (0,)), ((), ())), preferred_element_type=F32)
         teacher[b * 64:(b + 1) * 64, :] = (both[0:64] * 256.0 + both[64:128]) * (1.0 / 65536.0)
 
-    for copy in head_in:
-        copy.wait()
-    for copy in sib:
-        copy.wait_recv()
-
-    for n in range(5):
-        ns = slice(n * 256, (n + 1) * 256)
-        logits[:, ns] = lax.dot_general(
-            hid[...], head[ns, :], (((1,), (1,)), ((), ())), preferred_element_type=F32
-        )
-    lg = logits[...]
-    m_own = jnp.max(lg, axis=1, keepdims=True)
-    ex = jnp.exp(lg - m_own)
-    e_buf[...] = ex
-    s_own = jnp.sum(ex, axis=1, keepdims=True)
-    t_own = jnp.sum(teacher[...] * lg, axis=1, keepdims=True)
-    my_row = blk * 4
-    row_id = iota((GRP, 128), 0)
-    lane = iota((GRP, 128), 1)
-    w_own = jnp.zeros((GRP, 128), F32)
-    for r in range(4):
-        w_own = jnp.where(row_id == my_row + r, weight[r], w_own)
-    wide = jnp.where(lane == 0, m_own, jnp.where(lane == 1, s_own, jnp.where(lane == 2, w_own, t_own)))
-    packet[...] = wide.T[0:8, :]
-
-    def combine(buf):
-        top = buf[0, 0:1, :]
-        for i in range(1, 8):
-            top = jnp.maximum(top, buf[i, 0:1, :])
-        total = [jnp.zeros((1, GRP), F32) for _ in range(3)]
-        for i in range(8):
-            total[0] = total[0] + buf[i, 1:2, :] * jnp.exp(buf[i, 0:1, :] - top)
-            total[1] = total[1] + buf[i, 2:3, :]
-            total[2] = total[2] + buf[i, 3:4, :]
-        sub = iota((8, GRP), 0)
-        return jnp.where(
-            sub == 0, top, jnp.where(sub == 1, total[0], jnp.where(sub == 2, total[1], total[2]))
-        )
-
-    place = x * 2 + c
-    got = [
-        send(packet, st1.at[place], st1_s.at[i], st1_r.at[i], dev(dx=dx, dc=dc))
-        for i, (dx, dc) in enumerate(xc)
-    ]
-    st1[place] = packet[...]
-    for copy in got:
-        copy.wait_recv()
-    st2[z] = combine(st1)
-    mid = st2.at[z]
-    got = [send(mid, mid, st2_s.at[d - 1], st2_r.at[d - 1], dev(dz=d)) for d in range(1, NZ)]
+    t_own = jnp.sum(teacher[...] * logits[...], axis=1, keepdims=True)
+    packet2[...] = jnp.broadcast_to(t_own, (GRP, 128)).T[0:8, :]
     for copy in got:
         copy.wait_recv()
     final = combine(st2)
@@ -230,16 +262,25 @@
     scale = jnp.exp(m_own - top_c) / total_c
     g_buf[0] = (w_c * (e_buf[...] * scale - teacher[...])).astype(BF)
 
-    own_cols = cols[pl.ds(pl.multiple_of(my_row, 4), 4), :]
-    loss_out[...] = own_cols[:, 0:1] + jnp.log(own_cols[:, 1:2]) - own_cols[:, 3:4] + jnp.zeros((4, 128), F32)
-
     got_y = {}
     for k in range(YC):
         ks = pl.ds(k * YW, YW)
-        for d in (1, 3, 2):
-            got_y[d, k] = send(
+        for d in (1, 3):
+            got_y[d, k] = [send(
                 g_buf.at[0, :, ks], g_buf.at[d, :, ks], y_s.at[d - 1, k], y_r.at[d - 1, k], dev(dy=d)
-            )
+            )]
+
+    def forward(k):
+        ks = pl.ds(k * YW, YW)
+        got_y[2, k] = []
+        for d, n in ((1, 0), (3, 1)):
+            got_y[d, k].pop().wait_recv()
+            rows = pl.ds(n * 128, 128)
+            got_y[2, k].append(send(
+                g_buf.at[d, rows, ks], g_buf.at[2, rows, ks], f_s.at[n, k], f_r.at[n, k], dev(dy=d)
+            ))
+
+    got = over_xc(packet2, td1, td1_s, td1_r)
 
     i0 = iota((GRP, GRP), 0)
     src = ((i0 >> 7) << 7) + (((i0 >> 2) & 7) << 4) + (((i0 >> 5) & 3) << 2) + (i0 & 3)
@@ -296,7 +337,8 @@
             left = hid[:, pl.ds(pl.multiple_of(y * DS, DS), DS)]
         else:
             left = hy[d - 1]
-            got_y[d, k].wait_recv()
+            for copy in got_y[d, k]:
+                copy.wait_recv()
         term = lax.dot_general(
             left, g_buf[d, :, ks], (((0,), (0,)), ((), ())), preferred_element_type=F32
         )
@@ -315,6 +357,11 @@
     pair_stage(3)
     x_stage(2)
     x_stage(3)
+    forward(0)
+    for copy in got:
+        copy.wait_recv()
+    td2[z] = jnp.sum(td1[...], axis=0)
+    got = over_z(td2, td2_s, td2_r)
     got_hs = []
     for d in (1, 3, 2):
         got_hy[d].wait_recv()
@@ -323,8 +370,9 @@
     z_stage(0)
     z_stage(1)
     head_step(0, 0)
+    forward(1)
+    z_stage(2)
     head_step(0, 1)
-    z_stage(2)
     z_stage(3)
     for copy in got_hs:
         copy.wait_recv()
@@ -333,6 +381,15 @@
             head_step(d, k)
     for q in range(Q):
         last_stage(q)
+    for copy in got:
+        copy.wait_recv()
+    dots = jnp.concatenate([jnp.sum(td2[...], axis=0), jnp.zeros((120, GRP), F32)], axis=0).T
+    dot_buf[...] = dots
+    mine = pl.ds(pl.multiple_of(my_row, 4), 4)
+    own_cols = cols[mine, :]
+    own_loss = own_cols[:, 0:1] + jnp.log(own_cols[:, 1:2]) - dot_buf[mine, :][:, 0:1]
+    at_lane = iota((4, 128), 0) == iota((4, 128), 1)
+    loss_out[...] = jnp.sum(jnp.where(at_lane, own_loss, 0.0), axis=0, keepdims=True)
     outs = []
     for k in range(YC):
         head_step(2, k)
@@ -346,6 +403,21 @@
         copy.wait()
 
 
+def hand_out(row, loss, head, row_out, loss_out, head_out, buf, sem_in, sem_out):
+    parts = [pl.ds(i * (DS // 8), DS // 8) for i in range(8)]
+    ins = [pltpu.make_async_copy(head.at[p], buf.at[p], sem_in.at[i]) for i, p in enumerate(parts)]
+    outs = [pltpu.make_async_copy(buf.at[p], head_out.at[p], sem_out.at[i]) for i, p in enumerate(parts)]
+    for copy in ins:
+        copy.start()
+    row_out[...] = row[...]
+    loss_out[...] = loss[0, 0:4]
+    for arrive, leave in zip(ins, outs):
+        arrive.wait()
+        leave.start()
+    for copy in outs:
+        copy.wait()
+
+
 def shards(hidden, head, row_weight, teacher_ids, teacher_probs):
     dma = pltpu.SemaphoreType.DMA
     vm = pltpu.VMEM
@@ -355,15 +427,17 @@
         kernel,
         out_shape=(
             jax.ShapeDtypeStruct((4, D), BF),
-            jax.ShapeDtypeStruct((4, 128), F32),
+            jax.ShapeDtypeStruct((1, 128), F32),
             jax.ShapeDtypeStruct((DS, VOC), BF),
         ),
         in_specs=[vm_spec, any_spec, pl.BlockSpec(memory_space=pltpu.SMEM), vm_spec, vm_spec],
         out_specs=(vm_spec, vm_spec, any_spec),
         scratch_shapes=[
-            vm((VOC, D), BF), vm((16, QW), BF), vm((NX, 16, QW), BF), vm((GRP, D), BF),
+            vm((VOC, D), BF), vm((16, PW), BF), vm((16, PW), BF),
+            vm((NX, 16, PW), BF), vm((NX, NZ, 16, PW), BF), vm((GRP, D), BF),
             vm((8, 128), I32), vm((64, 8, 128), I32), vm((3, GRP, DS), BF),
             vm((GRP, VOC), F32), vm((GRP, VOC), F32), vm((GRP, VOC), F32),
+            vm((8, GRP), F32), vm((8, 8, GRP), F32), vm((8, 8, GRP), F32), vm((GRP, 128), F32),
             vm((8, GRP), F32), vm((8, 8, GRP), F32), vm((8, 8, GRP), F32), vm((GRP, 128), F32),
             vm((4, GRP, VOC), BF), vm((GRP, VOC), BF), vm((2, GRP, QW), F32),
             vm((Q, 128, QW), BF), vm((Q, 128, QW), BF), vm((Q, 128, QW), F32),
@@ -371,10 +445,11 @@
             vm((Q, NZ, 16, 256), F32), vm((Q, NZ, 16, 256), BF), vm((Q, NZ - 1, 16, 256), BF),
             vm((DS, VOC), F32), vm((DS, VOC), BF),
             dma((5,)), dma((YC,)),
-            dma((3,)), dma((3,)), dma((3,)), dma((3,)), dma((2, 4)), dma((2, 4)),
-            dma((7,)), dma((7,)), dma((8,)), dma((8,)), dma, dma,
+            dma((3,)), dma((3,)), dma((7,)), dma((7,)), dma((3,)), dma((3,)), dma((3,)), dma((3,)),
+            dma((2, 4)), dma((2, 4)), dma((7,)), dma((7,)), dma((16,)), dma((16,)), dma, dma,
             dma((3,)), dma((3,)), dma((3,)), dma((3,)), dma((7,)), dma((7,)), dma((7,)), dma((7,)),
-            dma((3, YC)), dma((3, YC)),
+            dma((7,)), dma((7,)), dma((7,)), dma((7,)),
+            dma((3, YC)), dma((3, YC)), dma((2, YC)), dma((2, YC)),
             dma((Q,)), dma((Q,)), dma((Q, 3)), dma((Q, 3)), dma((Q, 7)), dma((Q, 7)),
         ],
         compiler_params=pltpu.CompilerParams(
@@ -382,7 +457,17 @@
         ),
         cost_estimate=pl.CostEstimate(flops=8_100_000_000, bytes_accessed=14_000_000, transcendentals=330_000),
     )(hidden, head, row_weight, teacher_ids, teacher_probs)
-    return row_grad, loss[:, 0], head_grad
+    return pl.pallas_call(
+        hand_out,
+        out_shape=(
+            jax.ShapeDtypeStruct((4, D), BF),
+            jax.ShapeDtypeStruct((4,), F32),
+            jax.ShapeDtypeStruct((DS, VOC), BF),
+        ),
+        in_specs=[vm_spec, vm_spec, any_spec],
+        out_specs=(vm_spec, vm_spec, any_spec),
+        scratch_shapes=[vm((DS, VOC), BF), dma((8,)), dma((8,))],
+    )(row_grad, loss, head_grad)
 
 
 def solution(mesh):

time: 93.6 us -> 75.9 us (0.81)
  Pallas kernels: 86.6 us -> 74.7 us
  local copies, waits for them, and re-layouts: 6.09 us -> 0 us
    pallas_call x1, Pallas kernels: 86.6 us -> 70.7 us  [shards(): pl.pallas_call(kernel, out_shape=(jax.ShapeDtypeStruct((4, D), BF), jax.S...]
    unnamed x2 -> x0, local copies, waits for them, and re-layouts: 4.78 us -> none
    pallas_call x0 -> x1, Pallas kernels: none -> 3.97 us  [shards(): pl.pallas_call(hand_out, out_shape=(jax.ShapeDtypeStruct((4, D), BF), jax...]
    slice x1 -> x0, local copies, waits for them, and re-layouts: 1.3 us -> none  [shards(): return (row_grad, loss[:, 0], head_grad)]
where the time goes in v2:
time: 75.9 us; the launch traced here: 75.3 us
  Pallas kernels  74.7 us (98%)
    pallas_call x1, Pallas kernels, shards(): pl.pallas_call(kernel, out_shape=(jax.ShapeDtypeStruct((4, D), BF), jax.S...  70.7 us
    pallas_call x1, Pallas kernels, shards(): pl.pallas_call(hand_out, out_shape=(jax.ShapeDtypeStruct((4, D), BF), jax...  3.97 us

profile of v2, /device:TPU:2, one launch (start us, length us, event | category | flops | bytes accessed | tf_op | source)
XLA Modules:
  0.0 75.3 jit_solution(12976219701526281617)
XLA Ops:
  0.6 70.7 %shard_map.76 = (bf16[4,4096]{1,0:T(4,128)(2,1)}, f32[1,128]{1,0:T(1,128)}, bf16[1024,1280]{1,0:T(8,128)(2,1)}) custom-call(bf16[4,4096]{1,0:T(4,128)(2,1)} %hidden.1, bf16[1280,4096]{1,0:T(8,128)(2,1)} %head_hbm.1, f32[4]{0:T(128)} %weight.1, s32[4,128]{1,0:T(4,128)} %ids.1, s32[4,128]{1,0:T(4,128)} %probs.1), custom_call_target="tpu_custom_call" | custom-call | flops 8099999744 | bytes 14000000 | tf_op jit(solution)/shard_map/pallas_call | solution.py:426
  71.3 4.0 %shard_map.77 = (bf16[4,4096]{1,0:T(4,128)(2,1)}, f32[4]{0:T(128)}, bf16[1024,1280]{1,0:T(8,128)(2,1)}) custom-call(bf16[4,4096]{1,0:T(4,128)(2,1)} %get-tuple-element.6.row, f32[1,128]{1,0:T(1,128)} %get-tuple-element.7.loss, bf16[1024,1280]{1,0:T(8,128)(2,1)} %get-tuple-element.8.head), custom_call_target="tpu_custom_call" | custom-call | tf_op jit(solution)/shard_map/pallas_call | solution.py:460

commit v3 on v2

v3 whole, which is shorter than its diff:
```python
import jax
import jax.numpy as jnp
from jax import lax
from jax.experimental import pallas as pl
from jax.experimental.pallas import tpu as pltpu
from jax.sharding import PartitionSpec as P

MESH = pl.DeviceIdType.MESH
BF, F32, I32 = jnp.bfloat16, jnp.float32, jnp.int32
NZ, NX, NC, NY = 8, 4, 2, 4
D, VOC, TOPK = 4096, 1280, 128
GRP = 256
SLOTS = 16
DS = D // NY
CHUNKS = ((0, 1536), (1536, 1024), (2560, 1024), (3584, 512))
NQ = len(CHUNKS)
DH = D // 2
PW = DH // 4
RING = 1
RW = DH // RING
HW = DS // 4
YC = 2
YW = VOC // YC


def iota(shape, dim):
    return lax.broadcasted_iota(I32, shape, dim)


def kernel(
    hidden, head_hbm, weight, ids, probs,
    row_out, loss_out, head_out,
    head, own_a, own_b, own_h, buf_a, buf_b, buf_h, hid, meta_own, meta, hy,
    logits, teacher, lists, packet, st1, st2, cols, packet2, td1, td2, dot_buf, scales, scale_c,
    e_buf, grad, ep, tp, part1, part2, p1_send, p1_recv, p2_send, p2_recv,
    s1, x_send, x_recv, z_f32, z_send, z_recv,
    acc,
    sem_head,
    xa_s, xa_r, zb_s, zb_r, xb_s, xb_r, yh_s, yh_r, zh_s, zh_r, xh_s, xh_r, xm_s, xm_r, ring_s, ring_r, zm_s, zm_r,
    sib_s, sib_r, sm_s, sm_r,
    hs_s, hs_r, st1_s, st1_r, st2_s, st2_r, td1_s, td1_r, td2_s, td2_r,
    y_s, y_r, f_s, f_r, l_s, l_r, sc_s, sc_r,
    p1_s, p1_r, p2_s, p2_r, rx_s, rx_r, rz_s, rz_r,
):
    v, y = lax.axis_index("vocab"), lax.axis_index("rows")
    z, x, c = lax.div(v, 8), lax.rem(lax.div(v, 2), 4), lax.rem(v, 2)
    oc = 1 - c

    def dev(dz=0, dx=0, dc=0, dy=0):
        zz = lax.rem(z + dz, NZ)
        xx = lax.rem(x + dx, NX)
        cc = c if dc == 0 else oc
        return (zz * 8 + xx * 2 + cc, lax.rem(y + dy, NY))

    started = []

    def send(src, dst, ss, rs, to):
        copy = pltpu.make_async_remote_copy(
            src_ref=src, dst_ref=dst, send_sem=ss, recv_sem=rs, device_id=to, device_id_type=MESH
        )
        copy.start()
        started.append(copy)
        return copy

    head_in = []
    for i in range(5):
        part_rows = pl.ds(i * 256, 256)
        copy = pltpu.make_async_copy(head_hbm.at[part_rows], head.at[part_rows], sem_head.at[i])
        copy.start()
        head_in.append(copy)

    xc = [(dx, dc) for dx in range(NX) for dc in range(NC) if (dx, dc) != (0, 0)]
    barrier = pltpu.get_barrier_semaphore()
    peers = [dev(dx=dx, dc=dc) for dx, dc in xc]
    peers += [dev(dz=d) for d in range(1, NZ)]
    peers += [dev(dy=d) for d in range(1, NY)]
    for to in peers:
        pl.semaphore_signal(barrier, inc=1, device_id=to, device_id_type=MESH)

    h = hidden[...].astype(F32)
    for own, at in ((own_a, 0), (own_b, DH)):
        own[...] = jnp.concatenate(
            [h[:, at + i * PW:at + (i + 1) * PW] for i in range(4)], axis=0
        ).astype(BF)
    for d in (1, 3, 2):
        yy = lax.rem(y + d, NY)
        hs = hidden[:, pl.ds(pl.multiple_of(yy * DS, DS), DS)].astype(F32)
        own_h[d - 1] = jnp.concatenate([hs[:, i * HW:(i + 1) * HW] for i in range(4)], axis=0).astype(BF)
    meta_own[0:4, :] = ids[...]
    meta_own[4:8, :] = probs[...]
    pl.semaphore_wait(barrier, len(peers))

    got_a = [send(own_a, buf_a.at[x], xa_s.at[d - 1], xa_r.at[d - 1], dev(dx=d)) for d in (1, 3, 2)]
    got_b = [send(own_b, buf_b.at[x, z], zb_s.at[d - 1], zb_r.at[d - 1], dev(dz=d)) for d in range(1, NZ)]
    base = c * 8 + z
    blk = base * 4 + x
    got_m = [send(meta_own, meta.at[blk], xm_s.at[d - 1], xm_r.at[d - 1], dev(dx=d)) for d in (1, 3, 2)]
    got_h = [
        send(own_h.at[d - 1], buf_h.at[x, z, d - 1], yh_s.at[d - 1], yh_r.at[d - 1], dev(dy=d)) for d in (1, 3, 2)
    ]
    buf_a[x] = own_a[...]
    buf_b[x, z] = own_b[...]
    meta[blk] = meta_own[...]

    def rows_of(zz):
        return pl.ds(pl.multiple_of((c * 8 + zz) * 16, 16), 16)

    def lay_out(blocks, zz, at):
        blocks = [b.astype(F32) for b in blocks]
        for i in range(4):
            hid[rows_of(zz), at + i * PW:at + (i + 1) * PW] = jnp.concatenate(
                [b[4 * i:4 * i + 4] for b in blocks], axis=0
            ).astype(BF)

    sib = []

    def sib_send(zz, at):
        ref, n = hid.at[rows_of(zz), at:at + DH], len(sib)
        sib.append(send(ref, ref, sib_s.at[n], sib_r.at[n], dev(dc=1)))

    def ring_send(way, step):
        zz = lax.rem(z + (NZ - step if way == 0 else step), NZ)
        sent = []
        for n in range(RING):
            ref = hid.at[rows_of(zz), n * RW:(n + 1) * RW]
            sent.append(send(
                ref, ref, ring_s.at[way, step, n], ring_r.at[way, step, n], dev(dz=1 if way == 0 else NZ - 1)
            ))
        return sent

    got_xb = []

    def block_send(dz):
        zz = lax.rem(z + NZ - dz, NZ)
        if dz:
            got_b[dz - 1].wait_recv()
        ref = buf_b.at[x, zz]
        for d in (1, 3, 2):
            got_xb.append(send(ref, ref, xb_s.at[dz, d - 1], xb_r.at[dz, d - 1], dev(dx=d)))

    for copy in got_a:
        copy.wait_recv()
    lay_out([buf_a[i] for i in range(NX)], z, 0)
    now = [ring_send(0, 0), ring_send(1, 0)]
    sib_send(z, 0)
    for copy in got_m:
        copy.wait_recv()
    own_meta = meta.at[pl.ds((c * 8 + z) * 4, 4)]
    got_m = [send(own_meta, own_meta, zm_s.at[d - 1], zm_r.at[d - 1], dev(dz=d)) for d in range(1, NZ)]
    for step in range(1, 5):
        for way in range(2):
            if way == 1 and step == 4:
                continue
            for copy in now[way]:
                copy.wait_recv()
            if step < (4 if way == 0 else 3):
                now[way] = ring_send(way, step)
            sib_send(lax.rem(z + (NZ - step if way == 0 else step), NZ), 0)
        if step == 1:
            for copy in got_b:
                copy.wait_recv()
            mine = buf_b.at[x]
            for d in (1, 3, 2):
                got_xb.append(send(mine, mine, xb_s.at[0, d - 1], xb_r.at[0, d - 1], dev(dx=d)))
        if step == 2:
            for copy in got_h:
                copy.wait_recv()
            mine = buf_h.at[x, z]
            got_h = [send(mine, mine, zh_s.at[d - 1], zh_r.at[d - 1], dev(dz=d)) for d in range(1, NZ)]
    for copy in got_h:
        copy.wait_recv()
    mine = buf_h.at[x]
    got_h = [send(mine, mine, xh_s.at[d - 1], xh_r.at[d - 1], dev(dx=d)) for d in (1, 3, 2)]
    for copy in got_m:
        copy.wait_recv()
    half_meta = meta.at[pl.ds(c * 32, 32)]
    send(half_meta, half_meta, sm_s, sm_r, dev(dc=1)).wait_recv()

    for copy in got_xb:
        copy.wait_recv()
    for zz in range(NZ):
        lay_out([buf_b[i, zz] for i in range(NX)], zz, DH)
        sib_send(zz, DH)

    half = pl.ds(pl.multiple_of(c * 128, 128), 128)

    for copy in head_in:
        copy.wait()
    for copy in sib[:8]:
        copy.wait_recv()
    for n in range(5):
        ns = slice(n * 256, (n + 1) * 256)
        logits[:, ns] = lax.dot_general(
            hid[:, 0:DH], head[ns, 0:DH], (((1,), (1,)), ((), ())), preferred_element_type=F32
        )
    for copy in sib[8:]:
        copy.wait_recv()
    for n in range(5):
        ns = slice(n * 256, (n + 1) * 256)
        logits[:, ns] += lax.dot_general(
            hid[:, DH:D], head[ns, DH:D], (((1,), (1,)), ((), ())), preferred_element_type=F32
        )
    lg = logits[...]
    m_own = jnp.max(lg, axis=1, keepdims=True)
    ex = jnp.exp(lg - m_own)
    e_buf[0] = ex.astype(BF)
    s_own = jnp.sum(ex, axis=1, keepdims=True)
    my_row = blk * 4
    row_id = iota((GRP, 128), 0)
    lane = iota((GRP, 128), 1)
    w_own = jnp.zeros((GRP, 128), F32)
    for r in range(4):
        w_own = jnp.where(row_id == my_row + r, weight[r], w_own)
    wide = jnp.where(lane == 0, m_own, jnp.where(lane == 1, s_own, w_own))
    packet[...] = wide.T[0:8, :]

    def combine(buf):
        top = buf[0, 0:1, :]
        for i in range(1, 8):
            top = jnp.maximum(top, buf[i, 0:1, :])
        total = [jnp.zeros((1, GRP), F32) for _ in range(2)]
        for i in range(8):
            total[0] = total[0] + buf[i, 1:2, :] * jnp.exp(buf[i, 0:1, :] - top)
            total[1] = total[1] + buf[i, 2:3, :]
        sub = iota((8, GRP), 0)
        return jnp.where(sub == 0, top, jnp.where(sub == 1, total[0], total[1]))

    place = x * 2 + c

    def over_xc(own, buf, ss, rs):
        got = [
            send(own, buf.at[place], ss.at[i], rs.at[i], dev(dx=dx, dc=dc))
            for i, (dx, dc) in enumerate(xc)
        ]
        buf[place] = own[...]
        return got

    def over_z(buf, ss, rs):
        mid = buf.at[z]
        return [send(mid, mid, ss.at[d - 1], rs.at[d - 1], dev(dz=d)) for d in range(1, NZ)]

    got = over_xc(packet, st1, st1_s, st1_r)

    got_y = {}
    for k in range(YC):
        ks = pl.ds(k * YW, YW)
        for d in (1, 3):
            got_y[d, k] = [send(
                e_buf.at[0, :, ks], e_buf.at[d, :, ks], y_s.at[d - 1, k], y_r.at[d - 1, k], dev(dy=d)
            )]

    def forward(k):
        ks = pl.ds(k * YW, YW)
        got_y[2, k] = []
        for d, n in ((1, 0), (3, 1)):
            got_y[d, k].pop().wait_recv()
            rows = pl.ds(n * 128, 128)
            got_y[2, k].append(send(
                e_buf.at[d, rows, ks], e_buf.at[2, rows, ks], f_s.at[n, k], f_r.at[n, k], dev(dy=d)
            ))

    i0 = iota((GRP, GRP), 0)
    src = ((i0 >> 7) << 7) + (((i0 >> 2) & 7) << 4) + (((i0 >> 5) & 3) << 2) + (i0 & 3)
    perm = jnp.where(src == iota((GRP, GRP), 1), 1.0, 0.0).astype(BF)
    other = pl.ds(pl.multiple_of(oc * 128, 128), 128)
    got_p1, got_x, got_z = {}, {}, {}

    def pair_send(q, part, p_send, p_recv, ss, rs, left):
        at, width = CHUNKS[q]
        qs = slice(at, at + width)
        part[:, qs] = jnp.dot(left[...], head[:, qs], preferred_element_type=F32)
        p_send[:, qs] = part[other, qs].astype(BF)
        return send(p_send.at[:, qs], p_recv.at[:, qs], ss, rs, dev(dc=1))

    ep[...] = jnp.dot(perm, e_buf[0], preferred_element_type=F32).astype(BF)
    got_p1[0] = pair_send(0, part1, p1_send, p1_recv, p1_s.at[0], p1_r.at[0], ep)
    for copy in got:
        copy.wait_recv()
    st2[z] = combine(st1)
    got = over_z(st2, st2_s, st2_r)

    off = meta[:, 0:4, :].reshape(GRP, TOPK) - v * VOC
    prob = meta[:, 4:8, :].reshape(GRP, TOPK)
    mine = jnp.logical_and(off >= 0, off < VOC)
    mask = jnp.where(mine, 1.0, 0.0).astype(BF)
    before = jnp.where(iota((TOPK, TOPK), 0) < iota((TOPK, TOPK), 1), 1.0, 0.0).astype(BF)
    ri, rj = iota((GRP, GRP), 0), iota((GRP, GRP), 1)
    earlier = jnp.where(jnp.logical_and((ri >> 2) == (rj >> 2), rj < ri), 1.0, 0.0).astype(BF)
    count = jnp.dot(mask, jnp.ones((TOPK, TOPK), BF), preferred_element_type=F32).astype(BF)
    rank = jnp.dot(mask, before, preferred_element_type=F32)
    rank = rank + jnp.dot(earlier, count, preferred_element_type=F32)
    rank = jnp.where(mine, rank, -1.0).reshape(64, 4, TOPK)
    rows4 = iota((GRP, TOPK), 0) & 3
    code = (off * 4 + rows4).astype(F32).reshape(64, 4, TOPK)
    probf = prob.astype(F32).reshape(64, 4, TOPK)
    slot = iota((64, SLOTS, TOPK), 1)
    lane3 = iota((64, SLOTS, TOPK), 2)
    slot_f = slot.astype(F32)
    code_at = jnp.zeros((64, SLOTS, TOPK), F32)
    prob_at = jnp.zeros((64, SLOTS, TOPK), F32)
    for r in range(4):
        hit = rank[:, r:r + 1, :] == slot_f
        code_at = code_at + jnp.where(hit, code[:, r:r + 1, :], 0.0)
        prob_at = prob_at + jnp.where(hit, probf[:, r:r + 1, :], 0.0)
    code_c = jnp.sum(code_at, axis=2, keepdims=True)
    prob_c = jnp.sum(prob_at, axis=2, keepdims=True)
    lists[0] = jnp.sum(
        jnp.where(lane3 == slot, code_c, 0.0) + jnp.where(lane3 == slot + SLOTS, prob_c, 0.0), axis=1
    )
    got_l = {
        d: send(lists.at[0], lists.at[d], l_s.at[d - 1], l_r.at[d - 1], dev(dy=d)) for d in (1, 3, 2)
    }
    lanes = iota((256, 128), 1)
    places = iota((256, VOC), 1)
    block_row = (iota((256, 128), 0) >> 4) << 2

    def make_teacher(code_c, prob_c):
        code_i = code_c.reshape(64 * SLOTS, 1).astype(I32)
        prob_i = prob_c.reshape(64 * SLOTS, 1).astype(I32)
        for b in range(4):
            code_b, prob_b = code_i[b * 256:(b + 1) * 256], prob_i[b * 256:(b + 1) * 256]
            one_hot = jnp.where((code_b >> 2) == places, 1.0, 0.0).astype(BF)
            byte = jnp.where(lanes < 64, prob_b >> 8, prob_b & 255).astype(F32)
            at = jnp.where((lanes & 63) == block_row + (code_b & 3), byte, 0.0).astype(BF)
            both = lax.dot_general(at, one_hot, (((0,), (0,)), ((), ())), preferred_element_type=F32)
            teacher[b * 64:(b + 1) * 64, :] = (both[0:64] * 256.0 + both[64:128]) * (1.0 / 65536.0)

    def other_teacher(d):
        got_l[d].wait_recv()
        flat = jnp.broadcast_to(lists[d][:, None, :], (64, SLOTS, TOPK))
        make_teacher(
            jnp.sum(jnp.where(lane3 == slot, flat, 0.0), axis=2, keepdims=True),
            jnp.sum(jnp.where(lane3 == slot + SLOTS, flat, 0.0), axis=2, keepdims=True),
        )

    make_teacher(code_c, prob_c)
    tp[...] = jnp.dot(perm, teacher[...].astype(BF), preferred_element_type=F32).astype(BF)
    got_p2 = pair_send(0, part2, p2_send, p2_recv, p2_s, p2_r, tp)
    t_own = jnp.sum(teacher[...] * logits[...], axis=1, keepdims=True)
    packet2[...] = jnp.broadcast_to(t_own, (GRP, 128)).T[0:8, :]
    got_td = over_xc(packet2, td1, td1_s, td1_r)
    for copy in got:
        copy.wait_recv()

    final = combine(st2)
    top, ratio, w_row = final[0:1, :], final[2:3, :] / final[1:2, :], final[2:3, :]
    a_row = jnp.exp(packet[0:1, :] - top) * ratio
    b_row = jnp.exp(st1[x * 2 + oc, 0:1, :] - top) * ratio
    scales[0] = jnp.concatenate([a_row, w_row, b_row, final[0:2, :], jnp.zeros((3, GRP), F32)], axis=0)
    got_sc = {
        d: send(scales.at[0], scales.at[d], sc_s.at[d - 1], sc_r.at[d - 1], dev(dy=d)) for d in (1, 3, 2)
    }

    def columns(d):
        return jnp.concatenate([scales[d], jnp.zeros((120, GRP), F32)], axis=0).T

    cols[...] = columns(0)
    scale_c[...] = jnp.concatenate(
        [
            cols[i * 128 + k * 16 + j * 4:i * 128 + k * 16 + j * 4 + 4, :]
            for i in range(NC) for j in range(NX) for k in range(NZ)
        ],
        axis=0,
    )

    def x_stage(q):
        at, width = CHUNKS[q]
        qs = slice(at, at + width)
        got_p1[q].wait_recv()
        if q == 0:
            got_p2.wait_recv()
            sc = scale_c[half, :]
            total = sc[:, 0:1] * part1[half, qs] + sc[:, 2:3] * p1_recv[:, qs].astype(F32)
            total = total - sc[:, 1:2] * (part2[half, qs] + p2_recv[...].astype(F32))
        else:
            total = part1[half, qs] + p1_recv[:, qs].astype(F32)
        s1[:, qs] = total
        x_send[:, qs] = total.astype(BF)
        for d in (1, 3, 2):
            xx = lax.rem(x + d, NX)
            rows = pl.ds(pl.multiple_of(xx * 32, 32), 32)
            got_x[q, d] = send(
                x_send.at[rows, qs], x_recv.at[d - 1, :, qs], rx_s.at[q, d - 1], rx_r.at[q, d - 1], dev(dx=d)
            )

    def pair_stage(q):
        got_p1[q] = pair_send(q, part1, p1_send, p1_recv, p1_s.at[q], p1_r.at[q], ep)

    def z_stage(q):
        at, width = CHUNKS[q]
        qs = slice(at, at + width)
        w4 = width // 4
        zs = slice(at // 4, at // 4 + w4)
        for d in (1, 3, 2):
            got_x[q, d].wait_recv()
        s2 = s1[pl.ds(pl.multiple_of(x * 32, 32), 32), qs]
        for d in range(3):
            s2 = s2 + x_recv[d, :, qs].astype(F32)
        for zz in range(NZ):
            piece = jnp.concatenate([s2[4 * zz:4 * zz + 4, i * w4:(i + 1) * w4] for i in range(4)], axis=0)
            z_f32[zz, :, zs] = piece
            z_send[zz, :, zs] = piece.astype(BF)
        for d in range(1, NZ):
            zz = lax.rem(z + d, NZ)
            got_z[q, d] = send(
                z_send.at[zz, :, zs], z_recv.at[d - 1, :, zs], rz_s.at[q, d - 1], rz_r.at[q, d - 1], dev(dz=d)
            )

    def last_stage(q):
        at, width = CHUNKS[q]
        w4 = width // 4
        zs = slice(at // 4, at // 4 + w4)
        for d in range(1, NZ):
            got_z[q, d].wait_recv()
        total = z_f32[z, :, zs]
        for d in range(NZ - 1):
            total = total + z_recv[d, :, zs].astype(F32)
        row_out[:, at:at + width] = jnp.concatenate(
            [total[4 * i:4 * i + 4] for i in range(4)], axis=1
        ).astype(BF)

    def head_step(d, k):
        ks = slice(k * YW, (k + 1) * YW)
        if d == 0:
            left, sc = hid[:, pl.ds(pl.multiple_of(y * DS, DS), DS)], cols
        else:
            left, sc = hy[d - 1], scale_c
            for copy in got_y[d, k]:
                copy.wait_recv()
        grad[:, ks] = (sc[:, 0:1] * e_buf[d, :, ks].astype(F32) - sc[:, 1:2] * teacher[:, ks]).astype(BF)
        term = lax.dot_general(
            left, grad[:, ks], (((0,), (0,)), ((), ())), preferred_element_type=F32
        )
        if d == 0:
            acc[:, ks] = term
        elif d != 2:
            acc[:, ks] += term
        else:
            head_out[:, ks] = (acc[:, ks] + term).astype(BF)

    def prepare(d):
        other_teacher(d)
        got_sc[d].wait_recv()
        scale_c[...] = columns(d)

    x_stage(0)
    ep[...] = (scale_c[:, 0:1] * ep[...].astype(F32) - scale_c[:, 1:2] * tp[...].astype(F32)).astype(BF)
    pair_stage(1)
    pair_stage(2)
    x_stage(1)
    pair_stage(3)
    x_stage(2)
    x_stage(3)
    forward(0)
    for copy in got_h:
        copy.wait_recv()
    got_hs = []
    for d in (1, 3, 2):
        for zz in range(NZ):
            blocks = [buf_h[j, zz, d - 1].astype(F32) for j in range(NX)]
            for i in range(4):
                hy[d - 1, rows_of(zz), i * HW:(i + 1) * HW] = jnp.concatenate(
                    [b[4 * i:4 * i + 4] for b in blocks], axis=0
                ).astype(BF)
        ref = hy.at[d - 1, half]
        got_hs.append(send(ref, ref, hs_s.at[d - 1], hs_r.at[d - 1], dev(dc=1)))
    head_step(0, 0)
    head_step(0, 1)
    forward(1)
    for copy in got_td:
        copy.wait_recv()
    td2[z] = jnp.sum(td1[...], axis=0)
    got_td = over_z(td2, td2_s, td2_r)
    z_stage(0)
    for copy in got_hs:
        copy.wait_recv()
    prepare(1)
    head_step(1, 0)
    z_stage(1)
    head_step(1, 1)
    prepare(3)
    z_stage(2)
    head_step(3, 0)
    head_step(3, 1)
    z_stage(3)
    prepare(2)
    for k in range(YC):
        head_step(2, k)
    for q in range(NQ):
        last_stage(q)
    for copy in got_td:
        copy.wait_recv()
    dots = jnp.concatenate([jnp.sum(td2[...], axis=0), jnp.zeros((120, GRP), F32)], axis=0).T
    dot_buf[...] = dots
    mine = pl.ds(pl.multiple_of(my_row, 4), 4)
    own_cols = cols[mine, :]
    own_loss = own_cols[:, 3:4] + jnp.log(own_cols[:, 4:5]) - dot_buf[mine, :][:, 0:1]
    at_lane = iota((4, 128), 0) == iota((4, 128), 1)
    loss_out[...] = jnp.sum(jnp.where(at_lane, own_loss, 0.0), axis=0)[0:4]
    for copy in started:
        copy.wait_send()


def shards(hidden, head, row_weight, teacher_ids, teacher_probs):
    dma = pltpu.SemaphoreType.DMA
    vm = pltpu.VMEM
    any_spec = pl.BlockSpec(memory_space=pl.ANY)
    vm_spec = pl.BlockSpec(memory_space=pltpu.VMEM)
    return pl.pallas_call(
        kernel,
        out_shape=(
            vm((4, D), BF),
            vm((4,), F32),
            vm((DS, VOC), BF),
        ),
        in_specs=[vm_spec, any_spec, pl.BlockSpec(memory_space=pltpu.SMEM), vm_spec, vm_spec],
        out_specs=(vm_spec, vm_spec, vm_spec),
        scratch_shapes=[
            vm((VOC, D), BF), vm((16, PW), BF), vm((16, PW), BF), vm((3, 16, HW), BF),
            vm((NX, 16, PW), BF), vm((NX, NZ, 16, PW), BF), vm((NX, NZ, 3, 16, HW), BF), vm((GRP, D), BF),
            vm((8, 128), I32), vm((64, 8, 128), I32), vm((3, GRP, DS), BF),
            vm((GRP, VOC), F32), vm((GRP, VOC), F32), vm((4, 64, TOPK), F32),
            vm((8, GRP), F32), vm((8, 8, GRP), F32), vm((8, 8, GRP), F32), vm((GRP, 128), F32),
            vm((8, GRP), F32), vm((8, 8, GRP), F32), vm((8, 8, GRP), F32), vm((GRP, 128), F32),
            vm((4, 8, GRP), F32), vm((GRP, 128), F32),
            vm((4, GRP, VOC), BF), vm((GRP, VOC), BF), vm((GRP, VOC), BF), vm((GRP, VOC), BF),
            vm((GRP, D), F32), vm((GRP, CHUNKS[0][1]), F32),
            vm((128, D), BF), vm((128, D), BF), vm((128, CHUNKS[0][1]), BF), vm((128, CHUNKS[0][1]), BF),
            vm((128, D), F32), vm((128, D), BF), vm((3, 32, D), BF),
            vm((NZ, 16, D // 4), F32), vm((NZ, 16, D // 4), BF), vm((NZ - 1, 16, D // 4), BF),
            vm((DS, VOC), F32),
            dma((5,)),
            dma((3,)), dma((3,)), dma((7,)), dma((7,)), dma((1, 3)), dma((1, 3)),
            dma((3,)), dma((3,)), dma((7,)), dma((7,)), dma((3,)), dma((3,)), dma((3,)), dma((3,)),
            dma((2, 4, RING)), dma((2, 4, RING)), dma((7,)), dma((7,)), dma((16,)), dma((16,)), dma, dma,
            dma((3,)), dma((3,)), dma((7,)), dma((7,)), dma((7,)), dma((7,)),
            dma((7,)), dma((7,)), dma((7,)), dma((7,)),
            dma((3, YC)), dma((3, YC)), dma((2, YC)), dma((2, YC)),
            dma((3,)), dma((3,)), dma((3,)), dma((3,)),
            dma((NQ,)), dma((NQ,)), dma, dma, dma((NQ, 3)), dma((NQ, 3)), dma((NQ, 7)), dma((NQ, 7)),
        ],
        compiler_params=pltpu.CompilerParams(
            collective_id=0, has_side_effects=True, vmem_limit_bytes=52 << 20
        ),
        cost_estimate=pl.CostEstimate(flops=8_100_000_000, bytes_accessed=14_000_000, transcendentals=330_000),
    )(hidden, head, row_weight, teacher_ids, teacher_probs)


def solution(mesh):
    in_specs = (
        P(("vocab", "rows"), None),
        P("vocab", None),
        P(("vocab", "rows")),
        P(("vocab", "rows"), None),
        P(("vocab", "rows"), None),
    )
    out_specs = (P(("vocab", "rows"), None), P(("vocab", "rows")), P("rows", "vocab"))
    return jax.shard_map(shards, mesh=mesh, in_specs=in_specs, out_specs=out_specs, check_vma=False)
```

time: 75.9 us -> 70.8 us (0.933)
  Pallas kernels: 74.7 us -> 67.4 us
  local copies, waits for them, and re-layouts: 0 us -> 2.62 us
    pallas_call x2 -> x1, Pallas kernels: 74.7 us -> 67.4 us  [shards(): pl.pallas_call(kernel, out_shape=(vm((4, D), BF), vm((4,), F32), vm((DS,...]
    unnamed x0 -> x3, local copies, waits for them, and re-layouts: none -> 2.62 us
where the time goes in v3:
time: 70.8 us; the launch traced here: 70.7 us
  Pallas kernels  67.4 us (95%)
  local copies, waits for them, and re-layouts  2.62 us (4%)
    pallas_call x1, Pallas kernels, shards(): pl.pallas_call(kernel, out_shape=(vm((4, D), BF), vm((4,), F32), vm((DS,...  67.4 us
    unnamed x3, local copies, waits for them, and re-layouts  2.62 us

profile of v3, /device:TPU:2, one launch (start us, length us, event | category | flops | bytes accessed | tf_op | source)
XLA Modules:
  0.0 70.7 jit_solution(18193878477524277669)
XLA Ops:
  0.6 67.4 %shard_map.76 = (bf16[4,4096]{1,0:T(4,128)(2,1)S(1)}, f32[4]{0:T(128)S(1)}, bf16[1024,1280]{1,0:T(8,128)(2,1)S(1)}) custom-call(bf16[4,4096]{1,0:T(4,128)(2,1)} %hidden.1, bf16[1280,4096]{1,0:T(8,128)(2,1)} %head_hbm.1, f32[4]{0:T(128)} %weight.1, s32[4,128]{1,0:T(4,128)} %ids.1, s32[4,128]{1,0:T(4,128)} %probs.1), custom_call_target="tpu_custom_call" | custom-call | flops 8099999744 | bytes 14000000 | tf_op jit(solution)/shard_map/pallas_call | solution.py:509
  68.0 0.6 copy.11
  68.6 0.5 copy.12
  69.2 1.5 %copy.13 = bf16[1024,1280]{1,0:T(8,128)(2,1)} copy(bf16[1024,1280]{1,0:T(8,128)(2,1)S(1)} %get-tuple-element.5) | data formatting | bytes 5242880

commit v4 on v3

--- a/solution.py
+++ b/solution.py
@@ -19,8 +19,8 @@
 RING = 1
 RW = DH // RING
 HW = DS // 4
-YC = 2
-YW = VOC // YC
+YCH = ((0, 768), (768, 512))
+YC = len(YCH)
 
 
 def iota(shape, dim):
@@ -94,13 +94,14 @@
     got_b = [send(own_b, buf_b.at[x, z], zb_s.at[d - 1], zb_r.at[d - 1], dev(dz=d)) for d in range(1, NZ)]
     base = c * 8 + z
     blk = base * 4 + x
-    got_m = [send(meta_own, meta.at[blk], xm_s.at[d - 1], xm_r.at[d - 1], dev(dx=d)) for d in (1, 3, 2)]
+    mine = meta.at[c, x, z]
+    got_m = [send(meta_own, mine, zm_s.at[d - 1], zm_r.at[d - 1], dev(dz=d)) for d in range(1, NZ)]
     got_h = [
         send(own_h.at[d - 1], buf_h.at[x, z, d - 1], yh_s.at[d - 1], yh_r.at[d - 1], dev(dy=d)) for d in (1, 3, 2)
     ]
     buf_a[x] = own_a[...]
     buf_b[x, z] = own_b[...]
-    meta[blk] = meta_own[...]
+    meta[c, x, z] = meta_own[...]
 
     def rows_of(zz):
         return pl.ds(pl.multiple_of((c * 8 + zz) * 16, 16), 16)
@@ -143,10 +144,43 @@
     lay_out([buf_a[i] for i in range(NX)], z, 0)
     now = [ring_send(0, 0), ring_send(1, 0)]
     sib_send(z, 0)
-    for copy in got_m:
-        copy.wait_recv()
-    own_meta = meta.at[pl.ds((c * 8 + z) * 4, 4)]
-    got_m = [send(own_meta, own_meta, zm_s.at[d - 1], zm_r.at[d - 1], dev(dz=d)) for d in range(1, NZ)]
+    slot = iota((64, SLOTS, TOPK), 1)
+    lane3 = iota((64, SLOTS, TOPK), 2)
+    got_l = {}
+
+    def compact():
+        got_sm.wait_recv()
+        order = [(i, k, j) for i in range(NC) for j in range(NZ) for k in range(NX)]
+        off = jnp.concatenate([meta[o][0:4] for o in order], axis=0) - v * VOC
+        prob = jnp.concatenate([meta[o][4:8] for o in order], axis=0)
+        mine = jnp.logical_and(off >= 0, off < VOC)
+        mask = jnp.where(mine, 1.0, 0.0).astype(BF)
+        before = jnp.where(iota((TOPK, TOPK), 0) < iota((TOPK, TOPK), 1), 1.0, 0.0).astype(BF)
+        ri, rj = iota((GRP, GRP), 0), iota((GRP, GRP), 1)
+        earlier = jnp.where(jnp.logical_and((ri >> 2) == (rj >> 2), rj < ri), 1.0, 0.0).astype(BF)
+        count = jnp.dot(mask, jnp.ones((TOPK, TOPK), BF), preferred_element_type=F32).astype(BF)
+        rank = jnp.dot(mask, before, preferred_element_type=F32)
+        rank = rank + jnp.dot(earlier, count, preferred_element_type=F32)
+        rank = jnp.where(mine, rank, -1.0).reshape(64, 4, TOPK)
+        rows4 = iota((GRP, TOPK), 0) & 3
+        code = (off * 4 + rows4).astype(F32).reshape(64, 4, TOPK)
+        probf = prob.astype(F32).reshape(64, 4, TOPK)
+        slot_f = slot.astype(F32)
+        code_at = jnp.zeros((64, SLOTS, TOPK), F32)
+        prob_at = jnp.zeros((64, SLOTS, TOPK), F32)
+        for r in range(4):
+            hit = rank[:, r:r + 1, :] == slot_f
+            code_at = code_at + jnp.where(hit, code[:, r:r + 1, :], 0.0)
+            prob_at = prob_at + jnp.where(hit, probf[:, r:r + 1, :], 0.0)
+        code_c = jnp.sum(code_at, axis=2, keepdims=True)
+        prob_c = jnp.sum(prob_at, axis=2, keepdims=True)
+        lists[0] = jnp.sum(
+            jnp.where(lane3 == slot, code_c, 0.0) + jnp.where(lane3 == slot + SLOTS, prob_c, 0.0), axis=1
+        )
+        for d in (1, 3, 2):
+            got_l[d] = send(lists.at[0], lists.at[d], l_s.at[d - 1], l_r.at[d - 1], dev(dy=d))
+        return code_c, prob_c
+
     for step in range(1, 5):
         for way in range(2):
             if way == 1 and step == 4:
@@ -157,25 +191,31 @@
                 now[way] = ring_send(way, step)
             sib_send(lax.rem(z + (NZ - step if way == 0 else step), NZ), 0)
         if step == 1:
+            for copy in got_m:
+                copy.wait_recv()
+            mine = meta.at[c, x]
+            got_m = [send(mine, mine, xm_s.at[d - 1], xm_r.at[d - 1], dev(dx=d)) for d in (1, 3, 2)]
             for copy in got_b:
                 copy.wait_recv()
             mine = buf_b.at[x]
             for d in (1, 3, 2):
                 got_xb.append(send(mine, mine, xb_s.at[0, d - 1], xb_r.at[0, d - 1], dev(dx=d)))
         if step == 2:
+            for copy in got_m:
+                copy.wait_recv()
+            mine = meta.at[c]
+            got_sm = send(mine, mine, sm_s, sm_r, dev(dc=1))
+        if step == 2:
             for copy in got_h:
                 copy.wait_recv()
             mine = buf_h.at[x, z]
             got_h = [send(mine, mine, zh_s.at[d - 1], zh_r.at[d - 1], dev(dz=d)) for d in range(1, NZ)]
+        if step == 3:
+            code_c, prob_c = compact()
     for copy in got_h:
         copy.wait_recv()
     mine = buf_h.at[x]
     got_h = [send(mine, mine, xh_s.at[d - 1], xh_r.at[d - 1], dev(dx=d)) for d in (1, 3, 2)]
-    for copy in got_m:
-        copy.wait_recv()
-    half_meta = meta.at[pl.ds(c * 32, 32)]
-    send(half_meta, half_meta, sm_s, sm_r, dev(dc=1)).wait_recv()
-
     for copy in got_xb:
         copy.wait_recv()
     for zz in range(NZ):
@@ -242,15 +282,18 @@
     got = over_xc(packet, st1, st1_s, st1_r)
 
     got_y = {}
-    for k in range(YC):
-        ks = pl.ds(k * YW, YW)
+
+    def y_send(k):
+        ks = pl.ds(*YCH[k])
         for d in (1, 3):
             got_y[d, k] = [send(
                 e_buf.at[0, :, ks], e_buf.at[d, :, ks], y_s.at[d - 1, k], y_r.at[d - 1, k], dev(dy=d)
             )]
 
+    y_send(0)
+
     def forward(k):
-        ks = pl.ds(k * YW, YW)
+        ks = pl.ds(*YCH[k])
         got_y[2, k] = []
         for d, n in ((1, 0), (3, 1)):
             got_y[d, k].pop().wait_recv()
@@ -279,51 +322,20 @@
     st2[z] = combine(st1)
     got = over_z(st2, st2_s, st2_r)
 
-    off = meta[:, 0:4, :].reshape(GRP, TOPK) - v * VOC
-    prob = meta[:, 4:8, :].reshape(GRP, TOPK)
-    mine = jnp.logical_and(off >= 0, off < VOC)
-    mask = jnp.where(mine, 1.0, 0.0).astype(BF)
-    before = jnp.where(iota((TOPK, TOPK), 0) < iota((TOPK, TOPK), 1), 1.0, 0.0).astype(BF)
-    ri, rj = iota((GRP, GRP), 0), iota((GRP, GRP), 1)
-    earlier = jnp.where(jnp.logical_and((ri >> 2) == (rj >> 2), rj < ri), 1.0, 0.0).astype(BF)
-    count = jnp.dot(mask, jnp.ones((TOPK, TOPK), BF), preferred_element_type=F32).astype(BF)
-    rank = jnp.dot(mask, before, preferred_element_type=F32)
-    rank = rank + jnp.dot(earlier, count, preferred_element_type=F32)
-    rank = jnp.where(mine, rank, -1.0).reshape(64, 4, TOPK)
-    rows4 = iota((GRP, TOPK), 0) & 3
-    code = (off * 4 + rows4).astype(F32).reshape(64, 4, TOPK)
-    probf = prob.astype(F32).reshape(64, 4, TOPK)
-    slot = iota((64, SLOTS, TOPK), 1)
-    lane3 = iota((64, SLOTS, TOPK), 2)
-    slot_f = slot.astype(F32)
-    code_at = jnp.zeros((64, SLOTS, TOPK), F32)
-    prob_at = jnp.zeros((64, SLOTS, TOPK), F32)
-    for r in range(4):
-        hit = rank[:, r:r + 1, :] == slot_f
-        code_at = code_at + jnp.where(hit, code[:, r:r + 1, :], 0.0)
-        prob_at = prob_at + jnp.where(hit, probf[:, r:r + 1, :], 0.0)
-    code_c = jnp.sum(code_at, axis=2, keepdims=True)
-    prob_c = jnp.sum(prob_at, axis=2, keepdims=True)
-    lists[0] = jnp.sum(
-        jnp.where(lane3 == slot, code_c, 0.0) + jnp.where(lane3 == slot + SLOTS, prob_c, 0.0), axis=1
-    )
-    got_l = {
-        d: send(lists.at[0], lists.at[d], l_s.at[d - 1], l_r.at[d - 1], dev(dy=d)) for d in (1, 3, 2)
-    }
     lanes = iota((256, 128), 1)
     places = iota((256, VOC), 1)
     block_row = (iota((256, 128), 0) >> 4) << 2
 
-    def make_teacher(code_c, prob_c):
+    def make_teacher(code_c, prob_c, width):
         code_i = code_c.reshape(64 * SLOTS, 1).astype(I32)
         prob_i = prob_c.reshape(64 * SLOTS, 1).astype(I32)
         for b in range(4):
             code_b, prob_b = code_i[b * 256:(b + 1) * 256], prob_i[b * 256:(b + 1) * 256]
-            one_hot = jnp.where((code_b >> 2) == places, 1.0, 0.0).astype(BF)
+            one_hot = jnp.where((code_b >> 2) == places[:, 0:width], 1.0, 0.0).astype(BF)
             byte = jnp.where(lanes < 64, prob_b >> 8, prob_b & 255).astype(F32)
             at = jnp.where((lanes & 63) == block_row + (code_b & 3), byte, 0.0).astype(BF)
             both = lax.dot_general(at, one_hot, (((0,), (0,)), ((), ())), preferred_element_type=F32)
-            teacher[b * 64:(b + 1) * 64, :] = (both[0:64] * 256.0 + both[64:128]) * (1.0 / 65536.0)
+            teacher[b * 64:(b + 1) * 64, 0:width] = (both[0:64] * 256.0 + both[64:128]) * (1.0 / 65536.0)
 
     def other_teacher(d):
         got_l[d].wait_recv()
@@ -331,9 +343,10 @@
         make_teacher(
             jnp.sum(jnp.where(lane3 == slot, flat, 0.0), axis=2, keepdims=True),
             jnp.sum(jnp.where(lane3 == slot + SLOTS, flat, 0.0), axis=2, keepdims=True),
+            YCH[0][1],
         )
 
-    make_teacher(code_c, prob_c)
+    make_teacher(code_c, prob_c, VOC)
     tp[...] = jnp.dot(perm, teacher[...].astype(BF), preferred_element_type=F32).astype(BF)
     got_p2 = pair_send(0, part2, p2_send, p2_recv, p2_s, p2_r, tp)
     t_own = jnp.sum(teacher[...] * logits[...], axis=1, keepdims=True)
@@ -420,17 +433,22 @@
         ).astype(BF)
 
     def head_step(d, k):
-        ks = slice(k * YW, (k + 1) * YW)
+        at, width = YCH[k]
+        ks = slice(at, at + width)
         if d == 0:
             left, sc = hid[:, pl.ds(pl.multiple_of(y * DS, DS), DS)], cols
         else:
             left, sc = hy[d - 1], scale_c
             for copy in got_y[d, k]:
                 copy.wait_recv()
-        grad[:, ks] = (sc[:, 0:1] * e_buf[d, :, ks].astype(F32) - sc[:, 1:2] * teacher[:, ks]).astype(BF)
-        term = lax.dot_general(
-            left, grad[:, ks], (((0,), (0,)), ((), ())), preferred_element_type=F32
-        )
+        if k == 0:
+            grad[...] = (
+                sc[:, 0:1] * e_buf[d, :, ks].astype(F32) - sc[:, 1:2] * teacher[:, ks]
+            ).astype(BF)
+            right = grad[...]
+        else:
+            right = e_buf[d, :, ks]
+        term = lax.dot_general(left, right, (((0,), (0,)), ((), ())), preferred_element_type=F32)
         if d == 0:
             acc[:, ks] = term
         elif d != 2:
@@ -444,6 +462,11 @@
         scale_c[...] = columns(d)
 
     x_stage(0)
+    late = slice(YCH[1][0], YCH[1][0] + YCH[1][1])
+    e_buf[0, :, late] = (
+        cols[:, 0:1] * e_buf[0, :, late].astype(F32) - cols[:, 1:2] * teacher[:, late]
+    ).astype(BF)
+    y_send(1)
     ep[...] = (scale_c[:, 0:1] * ep[...].astype(F32) - scale_c[:, 1:2] * tp[...].astype(F32)).astype(BF)
     pair_stage(1)
     pair_stage(2)
@@ -452,6 +475,12 @@
     x_stage(2)
     x_stage(3)
     forward(0)
+    head_step(0, 0)
+    head_step(0, 1)
+    for copy in got_td:
+        copy.wait_recv()
+    td2[z] = jnp.sum(td1[...], axis=0)
+    got_td = over_z(td2, td2_s, td2_r)
     for copy in got_h:
         copy.wait_recv()
     got_hs = []
@@ -464,23 +493,17 @@
                 ).astype(BF)
         ref = hy.at[d - 1, half]
         got_hs.append(send(ref, ref, hs_s.at[d - 1], hs_r.at[d - 1], dev(dc=1)))
-    head_step(0, 0)
-    head_step(0, 1)
-    forward(1)
-    for copy in got_td:
-        copy.wait_recv()
-    td2[z] = jnp.sum(td1[...], axis=0)
-    got_td = over_z(td2, td2_s, td2_r)
     z_stage(0)
+    prepare(1)
     for copy in got_hs:
         copy.wait_recv()
-    prepare(1)
     head_step(1, 0)
     z_stage(1)
+    prepare(3)
+    head_step(3, 0)
+    z_stage(2)
+    forward(1)
     head_step(1, 1)
-    prepare(3)
-    z_stage(2)
-    head_step(3, 0)
     head_step(3, 1)
     z_stage(3)
     prepare(2)
@@ -518,12 +541,12 @@
         scratch_shapes=[
             vm((VOC, D), BF), vm((16, PW), BF), vm((16, PW), BF), vm((3, 16, HW), BF),
             vm((NX, 16, PW), BF), vm((NX, NZ, 16, PW), BF), vm((NX, NZ, 3, 16, HW), BF), vm((GRP, D), BF),
-            vm((8, 128), I32), vm((64, 8, 128), I32), vm((3, GRP, DS), BF),
+            vm((8, 128), I32), vm((NC, NX, NZ, 8, 128), I32), vm((3, GRP, DS), BF),
             vm((GRP, VOC), F32), vm((GRP, VOC), F32), vm((4, 64, TOPK), F32),
             vm((8, GRP), F32), vm((8, 8, GRP), F32), vm((8, 8, GRP), F32), vm((GRP, 128), F32),
             vm((8, GRP), F32), vm((8, 8, GRP), F32), vm((8, 8, GRP), F32), vm((GRP, 128), F32),
             vm((4, 8, GRP), F32), vm((GRP, 128), F32),
-            vm((4, GRP, VOC), BF), vm((GRP, VOC), BF), vm((GRP, VOC), BF), vm((GRP, VOC), BF),
+            vm((4, GRP, VOC), BF), vm((GRP, YCH[0][1]), BF), vm((GRP, VOC), BF), vm((GRP, VOC), BF),
             vm((GRP, D), F32), vm((GRP, CHUNKS[0][1]), F32),
             vm((128, D), BF), vm((128, D), BF), vm((128, CHUNKS[0][1]), BF), vm((128, CHUNKS[0][1]), BF),
             vm((128, D), F32), vm((128, D), BF), vm((3, 32, D), BF),

time: 70.8 us -> 69 us (0.975)
  the two profiles are of different devices: /device:TPU:2 before, /device:TPU:24 now
where the time goes in v4:
time: 69 us; the launch traced here: 68.9 us
  Pallas kernels  65.6 us (95%)
  local copies, waits for them, and re-layouts  2.62 us (4%)
    pallas_call x1, Pallas kernels, shards(): pl.pallas_call(kernel, out_shape=(vm((4, D), BF), vm((4,), F32), vm((DS,...  65.6 us
    unnamed x3, local copies, waits for them, and re-layouts  2.62 us

profile of v4, /device:TPU:24, one launch (start us, length us, event | category | flops | bytes accessed | tf_op | source)
XLA Modules:
  0.0 68.9 jit_solution(5701808861607912567)
XLA Ops:
  0.6 65.6 %shard_map.76 = (bf16[4,4096]{1,0:T(4,128)(2,1)S(1)}, f32[4]{0:T(128)S(1)}, bf16[1024,1280]{1,0:T(8,128)(2,1)S(1)}) custom-call(bf16[4,4096]{1,0:T(4,128)(2,1)} %hidden.1, bf16[1280,4096]{1,0:T(8,128)(2,1)} %head_hbm.1, f32[4]{0:T(128)} %weight.1, s32[4,128]{1,0:T(4,128)} %ids.1, s32[4,128]{1,0:T(4,128)} %probs.1), custom_call_target="tpu_custom_call" | custom-call | flops 8099999744 | bytes 14000000 | tf_op jit(solution)/shard_map/pallas_call | solution.py:532
  66.2 0.6 copy.11
  66.9 0.5 copy.12
  67.4 1.5 %copy.13 = bf16[1024,1280]{1,0:T(8,128)(2,1)} copy(bf16[1024,1280]{1,0:T(8,128)(2,1)S(1)} %get-tuple-element.5) | data formatting | bytes 5242880
